TPU v7x, 128 devices: a whole 4x4x4 slice. The times are simulated.
128 devices in a mesh: vp: 16 (over z, y), op: 8 (over x, core).
Axes of the slice: x: 4, y: 4, z: 4, core: 2. Of those that a mesh axis runs over, the one named last changes fastest.
Arguments:
- amplitudes: bfloat16 [16384, 16384], P('vp', 'op'), may hold values from -6 to 6
- integrals: bfloat16 [16, 16384, 2048], P('vp', 'op'), may hold values from -0.046875 to 0.046875
- pair_class: int32 [16384, 1], P('vp'), may hold values from 0 to 15; in each aligned block of 1024 rows (0 to 1023, 1024 to 2047, ...) at most 160 rows name the same one
Outputs:
- ladder: bfloat16 [2048, 16384], P('op', 'vp')
Inputs may be any that keep to these rules, and one draw needn't show every extreme that they name: `pair_class`: in each aligned block of 1024 rows (the rows of one index of vp) no class is named by more than 160 rows; some class is named by exactly 160 rows of some block.
All inputs are finite; a program needn't handle non-finite values.
Results may differ from a plain program's by a relative error of at most 0.017.
Values may be sent and summed in bfloat16 or wider, within the bound.
No kernel may reach another device: no remote copies, remote signals or barrier semaphores. Data moves between devices by JAX's collectives and lax.ppermute only.
A program may use at most 64 MiB of HBM per device.

v0:
```python
import jax
import jax.numpy as jnp
from jax import lax
from jax.sharding import PartitionSpec as P


def place_rows(classes, n_class, capacity):
    onehot = (classes[:, None] == jnp.arange(n_class, dtype=jnp.int32)[None, :]).astype(jnp.int32)
    before = jnp.cumsum(onehot, axis=0)
    position = jnp.sum(before * onehot, axis=1) - 1
    return classes * capacity + position


def ladder_sums(arrived, w_local):
    n_source = arrived.shape[0]
    per_source = arrived.shape[1]
    stacked = arrived.reshape(n_source * per_source, arrived.shape[2])
    ab_rows = w_local.shape[1] // lax.axis_size("op")
    summed = lax.psum_scatter(
        lax.dot_general(
            w_local, stacked, (((0,), (1,)), ((), ())), preferred_element_type=jnp.float32
        ).astype(jnp.bfloat16),
        "op",
        scatter_dimension=0,
        tiled=True,
    )
    values = summed.reshape(ab_rows, n_source, per_source)
    return lax.all_to_all(values, "vp", split_axis=1, concat_axis=1, tiled=True)


def local(amplitudes, integrals, pair_class):
    classes = pair_class[:, 0]
    n_class = lax.axis_size("vp")
    row_count = amplitudes.shape[0]
    capacity = row_count * 5 // 32
    slot_count = n_class * capacity
    w_local = integrals[0]
    slot_index = place_rows(classes, n_class, capacity)
    source_row = (
        jnp.zeros((slot_count,), jnp.int32)
        .at[slot_index]
        .set(jnp.arange(row_count, dtype=jnp.int32))
    )
    filled = (
        jnp.zeros((slot_count,), jnp.bfloat16)
        .at[slot_index]
        .set(jnp.ones((row_count,), jnp.bfloat16))
    )
    outgoing = (amplitudes[source_row] * filled[:, None]).reshape(
        n_class, capacity, amplitudes.shape[1]
    )
    received = lax.all_to_all(outgoing, "vp", split_axis=0, concat_axis=0, tiled=True)
    returned = ladder_sums(received, w_local)
    flat_back = returned.reshape(returned.shape[0], slot_count)
    return flat_back[:, slot_index]


def solution(mesh):
    return jax.shard_map(
        local,
        mesh=mesh,
        in_specs=(P("vp", "op"), P("vp", "op", None), P("vp", None)),
        out_specs=P("op", "vp"),
        check_vma=False,
    )
```

profile of v0, /device:TPU:0, one launch (start us, length us, event | category | flops | bytes accessed | tf_op | source)
XLA Modules:
  0.0 303.9 jit_solution(12629936160746971871)
XLA Ops:
  6.5 0.0 reduce-scatter.2.cloned.1.call-start
  6.5 0.7 fusion.4
  7.2 4.5 %reduce-window.6 = s32[16,8,128]{2,1,0:T(8,128)S(1)} reduce-window(s32[16,8,128]{2,1,0:T(8,128)S(1)} %fusion.4, s32[]{:T(128)} %constant.7.clone.1), window={size=1x1x128 pad=0_0x0_0x127_0}, to_apply=%region_0.0 | reduce-window | flops 2080768 | bytes 131076 | tf_op jit(solution)/shard_map/reduce-window
  11.7 0.1 slice.12
  11.8 0.1 copy.4
  12.0 0.1 copy.5
  12.0 0.1 broadcast_add_fusion
  12.1 0.7 fusion.3
  12.9 0.7 compare_select_fusion.1
  13.6 7.6 %scatter_custom_fusion.1 = bf16[2560]{0:T(1024)(128)(2,1)S(1)} fusion(s32[1024]{0:T(1024)S(1)} %bitcast.40, bf16[1024]{0:T(1024)(128)(2,1)S(1)} %broadcast.46, bf16[]{:T(256)} %constant.6.clone.1), kind=kCustom, calls=%fused_computation.20 | custom fusion | bytes 5122 | tf_op jit(solution)/shard_map/scatter | solution.py:47
  21.2 0.1 mul.24
  21.3 4.3 %scatter_custom_fusion = s32[2560]{0:T(1024)S(1)} fusion(s32[1024]{0:T(1024)S(1)} %bitcast.41, s32[1024]{0:T(1024)S(1)} %iota.11, s32[]{:T(128)} %constant.7.clone.1), kind=kCustom, calls=%fused_computation.18 | custom fusion | bytes 10244 | tf_op jit(solution)/shard_map/scatter | solution.py:42
  25.6 22.9 %gather_fusion = bf16[2560,2048]{1,0:T(8,128)(2,1)} fusion(bf16[1024,2048]{1,0:T(8,128)(2,1)} %param.3, s32[3072]{0:T(1024)S(1)} %pad_clamp_fusion), kind=kCustom, calls=%fused_computation | custom fusion | bytes 20981760 | tf_op jit(solution)/shard_map/gather | solution.py:49
  48.5 5.7 %broadcast_multiply_fusion = bf16[16,160,2048]{2,1,0:T(8,128)(2,1)S(1)} fusion(bf16[16,160,2048]{2,1,0:T(8,128)(2,1)} %bitcast.31, bf16[16,160]{1,0:T(8,128)(2,1)S(1)} %mul.24), kind=kLoop, calls=%fused_computation.7 | loop fusion | flops 5242880 | bytes 20976640 | tf_op jit(solution)/shard_map/mul | solution.py:49
  54.2 0.0 copy-start
  54.2 126.5 %all_to_all.10 = bf16[16,160,2048]{2,1,0:T(8,128)(2,1)S(1)} all-to-all(bf16[16,160,2048]{2,1,0:T(8,128)(2,1)S(1)} %broadcast_multiply_fusion), channel_id=1, replica_groups=mesh['vp'=16,'op'=8] {'vp'}, dimensions={0} | all-to-all | bytes 20971520 | tf_op jit(solution)/shard_map/all_to_all | solution.py:52
  180.7 0.0 copy-done
  180.7 24.3 %fusion = bf16[2048,2560]{0,1:T(8,128)(2,1)} fusion(bf16[2560,2048]{1,0:T(8,128)(2,1)S(1)} %bitcast.33, bf16[1,2048,2048]{2,1,0:T(8,128)(2,1)S(1)} %copy-done), kind=kOutput, calls=%fused_computation.5 | convolution fusion | flops 21480079360 | bytes 29360128 | tf_op jit(solution)/shard_map/dot_general | solution.py:20
  205.0 0.0 reduce-scatter.2.cloned.1.call-update
  205.0 60.0 %reduce-scatter.2.cloned.1.call-done = bf16[256,2560]{0,1:T(8,128)(2,1)} async-done(((bf16[2048,2560]{0,1:T(8,128)(2,1)}), bf16[256,2560]{0,1:T(8,128)(2,1)}) %reduce-scatter.2.cloned.1.call-update) | async-done | bytes 1310736 | tf_op jit(solution)/shard_map/reduce_scatter | solution.py:19
  265.0 7.0 %all-to-all-start.1 = ((bf16[256,16,160]{0,2,1:T(8,128)(2,1)}), bf16[256,16,160]{0,2,1:T(8,128)(2,1)S(1)}, u32[]{:S(2)}, u32[]{:S(2)}) async-start(bf16[256,16,160]{0,2,1:T(8,128)(2,1)} %bitcast.35), calls=%async_computation.2 | async-start | bytes 2621440 | tf_op jit(solution)/shard_map/all_to_all | solution.py:28
  272.0 20.2 %all-to-all-done.1 = bf16[256,16,160]{0,2,1:T(8,128)(2,1)S(1)} async-done(((bf16[256,16,160]{0,2,1:T(8,128)(2,1)}), bf16[256,16,160]{0,2,1:T(8,128)(2,1)S(1)}, u32[]{:S(2)}, u32[]{:S(2)}) %all-to-all-start.1) | async-done | bytes 1310752 | tf_op jit(solution)/shard_map/all_to_all | solution.py:28
  292.1 3.9 %gather_fusion.1 = bf16[1024,256]{1,0:T(8,128)(2,1)S(1)} fusion(bf16[256,2560]{0,1:T(8,128)(2,1)S(1)} %bitcast.32, s32[1024]{0:T(1024)S(1)} %broadcast_clamp_fusion), kind=kCustom, calls=%fused_computation.1 | custom fusion | bytes 1052672 | tf_op jit(solution)/shard_map/gather | solution.py:55
  296.1 1.0 copy.6
  (8 shorter events, 0.1 us)
Async XLA Ops:
  6.5 258.5 %reduce-scatter.2.cloned.1.call-start = ((), (), s32[]{:S(2)}) async-start(), calls=%async_computation.3 | async-start | bytes 11796480 | tf_op jit(solution)/shard_map/reduce_scatter | solution.py:19
  54.2 126.5 %copy-start = (bf16[1,2048,2048]{2,1,0:T(8,128)(2,1)S(1)}, bf16[1,2048,2048]{2,1,0:T(8,128)(2,1)}, u32[]{:S(2)}) copy-start(bf16[1,2048,2048]{2,1,0:T(8,128)(2,1)} %param.4) | copy-start | bytes 25165828
  265.0 27.1 %all-to-all-start.1 = ((bf16[256,16,160]{0,2,1:T(8,128)(2,1)}), bf16[256,16,160]{0,2,1:T(8,128)(2,1)S(1)}, u32[]{:S(2)}, u32[]{:S(2)}) async-start(bf16[256,16,160]{0,2,1:T(8,128)(2,1)} %bitcast.35), calls=%async_computation.2 | async-start | bytes 2621440 | tf_op jit(solution)/shard_map/all_to_all | solution.py:28
Sparse Core Ops, SparseCore 0:
  205.1 59.8 reduce-scatter.1
where the time goes:
time: 306 us; the launch traced here: 304 us
  blocking collectives  126 us (41%)
  waiting for transfers between devices  80.2 us (26%)
  local copies, waits for them, and re-layouts  40.1 us (13%)
  matrix products  24.3 us (8%)
  between operations  13.5 us (4%)
  other arithmetic  12.4 us (4%)
  starting transfers between devices  6.96 us (2%)
    all_to_all x1, blocking collectives, local(): lax.all_to_all(outgoing, 'vp', split_axis=0, concat_axis=0, tiled=True)  126 us
    reduce_scatter x1, waiting for transfers between devices, ladder_sums(): lax.psum_scatter(lax.dot_general(w_local, stacked, (((0,), (1,)), ((), ()...  60 us
    dot_general x1, matrix products, ladder_sums(): lax.dot_general(w_local, stacked, (((0,), (1,)), ((), ())), preferred_ele...  24.3 us
    gather x1, local copies, waits for them, and re-layouts, local(): amplitudes[source_row] * filled[:, None]  22.9 us
    all_to_all x1, waiting for transfers between devices, ladder_sums(): return lax.all_to_all(values, 'vp', split_axis=1, concat_axis=1, tiled=True)  20.2 us
    scatter x1, local copies, waits for them, and re-layouts, local(): filled = jnp.zeros((slot_count,), jnp.bfloat16).at[slot_index].set(jnp.on...  7.59 us
    all_to_all x1, starting transfers between devices, ladder_sums(): return lax.all_to_all(values, 'vp', split_axis=1, concat_axis=1, tiled=True)  6.96 us
  transfers between devices with their start and end apart: 2, of which 2 were waited for; matrix products, arithmetic and copies ran while one was open for 0% of the time, Pallas kernels for 0%

commit v1 on v0

v1 whole, which is shorter than its diff:
```python
import jax
import jax.numpy as jnp
from jax import lax
from jax.sharding import PartitionSpec as P

CHUNKS = (32, 32, 32, 32, 32)


def row_positions(classes, n_class):
    rows = classes.shape[1]
    onehot = (classes == lax.broadcasted_iota(jnp.int32, (n_class, rows), 0)).astype(jnp.bfloat16)
    upto = (
        lax.broadcasted_iota(jnp.int32, (rows, rows), 0)
        <= lax.broadcasted_iota(jnp.int32, (rows, rows), 1)
    ).astype(jnp.bfloat16)
    before = jnp.dot(onehot, upto, preferred_element_type=jnp.float32)
    position = jnp.sum(before * onehot.astype(jnp.float32), axis=0, keepdims=True)
    return position.astype(jnp.int32) - 1


def local(amplitudes, integrals, pair_class):
    n_class = lax.axis_size("vp")
    n_op = lax.axis_size("op")
    rows, depth = amplitudes.shape
    w = integrals[0]
    ab = w.shape[1]
    classes = pair_class.reshape(1, rows)
    position = row_positions(classes, n_class)
    out = jnp.zeros((ab // n_op, rows), jnp.float32)
    first = 0
    for size in CHUNKS:
        slot = jnp.where(
            (position >= first) & (position < first + size), classes * size + position - first, -1
        )
        pick = (slot == lax.broadcasted_iota(jnp.int32, (n_class * size, rows), 0)).astype(jnp.bfloat16)
        sent = jnp.dot(pick, amplitudes, preferred_element_type=jnp.float32).astype(jnp.bfloat16)
        got = lax.all_to_all(
            sent.reshape(n_class, size, depth), "vp", split_axis=0, concat_axis=0, tiled=True
        )
        partial = jnp.dot(
            got.reshape(n_class * size, depth), w, preferred_element_type=jnp.float32
        ).astype(jnp.bfloat16)
        summed = lax.psum_scatter(partial, "op", scatter_dimension=1, tiled=True)
        back = lax.all_to_all(
            summed.reshape(n_class, size, ab // n_op), "vp", split_axis=0, concat_axis=0, tiled=True
        )
        out = out + lax.dot_general(
            back.reshape(n_class * size, ab // n_op), pick, (((0,), (0,)), ((), ())),
            preferred_element_type=jnp.float32,
        )
        first += size
    return out.astype(jnp.bfloat16)


def solution(mesh):
    return jax.shard_map(
        local,
        mesh=mesh,
        in_specs=(P("vp", "op"), P("vp", "op", None), P("vp", None)),
        out_specs=P("op", "vp"),
        check_vma=False,
    )
```

time: 306 us -> 298 us (0.974)
  matrix products: 24.3 us -> 72.9 us
  waiting for transfers between devices: 80.2 us -> 39.2 us
  local copies, waits for them, and re-layouts: 40.1 us -> 0.01 us
  blocking collectives: 126 us -> 152 us
  starting transfers between devices: 6.96 us -> 18.7 us
  other arithmetic: 12.4 us -> 0.78 us
    reduce_scatter x1 -> x5, waiting for transfers between devices: 60 us -> 0.1 us  [local(): summed = lax.psum_scatter(partial, 'op', scatter_dimension=1, tiled=True)]
    dot_general x1 -> x16, matrix products: 24.3 us -> 72.9 us  [the longest x5 42.3 us: local(): jnp.dot(got.reshape(n_class * size, depth), w, preferred_element_type=jnp...]
    gather x3 -> x0, local copies, waits for them, and re-layouts: 27.8 us -> none  [the longest x1 22.9 us: local(): amplitudes[source_row] * filled[:, None]]
    all_to_all x1 -> x5, blocking collectives: 126 us -> 152 us  [local(): lax.all_to_all(sent.reshape(n_class, size, depth), 'vp', split_axis=0, co...]
    all_to_all x1 -> x5, waiting for transfers between devices: 20.2 us -> 39.1 us  [local(): lax.all_to_all(summed.reshape(n_class, size, ab // n_op), 'vp', split_axi...]
    scatter x2 -> x0, local copies, waits for them, and re-layouts: 11.9 us -> none  [the longest x1 7.59 us: local(): filled = jnp.zeros((slot_count,), jnp.bfloat16).at[slot_index].set(jnp.on...]
    all_to_all x1 -> x5, starting transfers between devices: 6.96 us -> 18.5 us  [local(): lax.all_to_all(summed.reshape(n_class, size, ab // n_op), 'vp', split_axi...]
    mul x1 -> x0, other arithmetic: 5.65 us -> none  [local(): amplitudes[source_row] * filled[:, None]]
  transfers between devices with their start and end apart: 2 -> 10, of which waited for: 2 -> 5; matrix products, arithmetic and copies ran while one was open for 0% -> 20% of each run, Pallas kernels for 0% -> 0%
where the time goes in v1:
time: 298 us; the launch traced here: 297 us
  blocking collectives  152 us (51%)
  matrix products  72.9 us (24%)
  waiting for transfers between devices  39.2 us (13%)
  starting transfers between devices  18.7 us (6%)
  between operations  13.3 us (4%)
    all_to_all x5, blocking collectives, local(): lax.all_to_all(sent.reshape(n_class, size, depth), 'vp', split_axis=0, co...  152 us
    dot_general x5, matrix products, local(): jnp.dot(got.reshape(n_class * size, depth), w, preferred_element_type=jnp...  42.3 us
    all_to_all x5, waiting for transfers between devices, local(): lax.all_to_all(summed.reshape(n_class, size, ab // n_op), 'vp', split_axi...  39.1 us
    dot_general x5, matrix products, local(): jnp.dot(pick, amplitudes, preferred_element_type=jnp.float32)  22.8 us
    all_to_all x5, starting transfers between devices, local(): lax.all_to_all(summed.reshape(n_class, size, ab // n_op), 'vp', split_axi...  18.5 us
    dot_general x5, matrix products, local(): lax.dot_general(back.reshape(n_class * size, ab // n_op), pick, (((0,), (...  6.65 us
  transfers between devices with their start and end apart: 10, of which 5 were waited for; matrix products, arithmetic and copies ran while one was open for 20% of the time, Pallas kernels for 0%

profile of v1, /device:TPU:0, one launch (start us, length us, event | category | flops | bytes accessed | tf_op | source)
XLA Modules:
  0.0 297.4 jit_solution(8262814488864570345)
XLA Ops:
  8.5 4.7 %convolution_convert_fusion = bf16[512,2048]{1,0:T(8,128)(2,1)S(1)} fusion(bf16[1024,2048]{1,0:T(8,128)(2,1)} %param.3, s32[1024]{0:T(1024)S(1)} %get-tuple-element.6), kind=kOutput, calls=%fused_computation.12 | convolution fusion | flops 2149056512 | bytes 6295552 | tf_op jit(solution)/shard_map/dot_general | solution.py:36
  13.2 36.3 %all_to_all.50 = bf16[16,32,2048]{2,1,0:T(8,128)(2,1)S(1)} all-to-all(bf16[16,32,2048]{2,1,0:T(8,128)(2,1)S(1)} %bitcast.62), channel_id=1, replica_groups=mesh['vp'=16,'op'=8] {'vp'}, dimensions={0} | all-to-all | bytes 4194304 | tf_op jit(solution)/shard_map/all_to_all | solution.py:37
  49.5 5.8 %fusion.23 = bf16[512,2048]{1,0:T(8,128)(2,1)} fusion(bf16[512,2048]{1,0:T(8,128)(2,1)S(1)} %bitcast.57, bf16[1,2048,2048]{2,1,0:T(8,128)(2,1)S(1)} %bitcast.79), kind=kOutput, calls=%fused_computation.21 | convolution fusion | flops 4296015872 | bytes 12582912 | tf_op jit(solution)/shard_map/dot_general | solution.py:40
  55.4 4.5 %convolution_convert_fusion.3 = bf16[512,2048]{1,0:T(8,128)(2,1)S(1)} fusion(bf16[1024,2048]{1,0:T(8,128)(2,1)} %param.3, s32[1024]{0:T(1024)S(1)} %get-tuple-element.7), kind=kOutput, calls=%fused_computation.15 | convolution fusion | flops 2149056512 | bytes 6295552 | tf_op jit(solution)/shard_map/dot_general | solution.py:36
  59.9 30.7 %all_to_all.51 = bf16[16,32,2048]{2,1,0:T(8,128)(2,1)S(1)} all-to-all(bf16[16,32,2048]{2,1,0:T(8,128)(2,1)S(1)} %bitcast.63), channel_id=1, replica_groups=mesh['vp'=16,'op'=8] {'vp'}, dimensions={0} | all-to-all | bytes 4194304 | tf_op jit(solution)/shard_map/all_to_all | solution.py:37
  90.6 9.1 %fusion.14 = bf16[512,2048]{1,0:T(8,128)(2,1)} fusion(bf16[512,2048]{1,0:T(8,128)(2,1)S(1)} %bitcast.58, bf16[1,2048,2048]{2,1,0:T(8,128)(2,1)} %param.4), kind=kOutput, calls=%fused_computation.18 | convolution fusion | flops 4296015872 | bytes 12582912 | tf_op jit(solution)/shard_map/dot_general | solution.py:40
  99.7 4.5 %convolution_convert_fusion.1 = bf16[512,2048]{1,0:T(8,128)(2,1)S(1)} fusion(bf16[1024,2048]{1,0:T(8,128)(2,1)} %param.3, s32[1024]{0:T(1024)S(1)} %get-tuple-element.8), kind=kOutput, calls=%fused_computation.13 | convolution fusion | flops 2149056512 | bytes 6295552 | tf_op jit(solution)/shard_map/dot_general | solution.py:36
  104.3 29.5 %all_to_all.52 = bf16[16,32,2048]{2,1,0:T(8,128)(2,1)S(1)} all-to-all(bf16[16,32,2048]{2,1,0:T(8,128)(2,1)S(1)} %bitcast.64), channel_id=1, replica_groups=mesh['vp'=16,'op'=8] {'vp'}, dimensions={0} | all-to-all | bytes 4194304 | tf_op jit(solution)/shard_map/all_to_all | solution.py:37
  133.7 9.1 %fusion.20 = bf16[512,2048]{1,0:T(8,128)(2,1)} fusion(bf16[512,2048]{1,0:T(8,128)(2,1)S(1)} %bitcast.59, bf16[1,2048,2048]{2,1,0:T(8,128)(2,1)} %param.4), kind=kOutput, calls=%fused_computation.20 | convolution fusion | flops 4296015872 | bytes 12582912 | tf_op jit(solution)/shard_map/dot_general | solution.py:40
  142.9 4.5 %convolution_convert_fusion.2 = bf16[512,2048]{1,0:T(8,128)(2,1)S(1)} fusion(bf16[1024,2048]{1,0:T(8,128)(2,1)} %param.3, s32[1024]{0:T(1024)S(1)} %get-tuple-element.9), kind=kOutput, calls=%fused_computation.14 | convolution fusion | flops 2149056512 | bytes 6295552 | tf_op jit(solution)/shard_map/dot_general | solution.py:36
  147.5 28.2 %all_to_all.53 = bf16[16,32,2048]{2,1,0:T(8,128)(2,1)S(1)} all-to-all(bf16[16,32,2048]{2,1,0:T(8,128)(2,1)S(1)} %bitcast.65), channel_id=1, replica_groups=mesh['vp'=16,'op'=8] {'vp'}, dimensions={0} | all-to-all | bytes 4194304 | tf_op jit(solution)/shard_map/all_to_all | solution.py:37
  175.7 9.2 %fusion.17 = bf16[512,2048]{1,0:T(8,128)(2,1)} fusion(bf16[512,2048]{1,0:T(8,128)(2,1)S(1)} %bitcast.60, bf16[1,2048,2048]{2,1,0:T(8,128)(2,1)} %param.4), kind=kOutput, calls=%fused_computation.19 | convolution fusion | flops 4296015872 | bytes 12582912 | tf_op jit(solution)/shard_map/dot_general | solution.py:40
  184.9 4.5 %convolution_convert_fusion.4 = bf16[512,2048]{1,0:T(8,128)(2,1)S(1)} fusion(bf16[1024,2048]{1,0:T(8,128)(2,1)} %param.3, s32[1024]{0:T(1024)S(1)} %get-tuple-element.5), kind=kOutput, calls=%fused_computation.16 | convolution fusion | flops 2149056512 | bytes 6295552 | tf_op jit(solution)/shard_map/dot_general | solution.py:36
  189.4 27.8 %all_to_all.54 = bf16[16,32,2048]{2,1,0:T(8,128)(2,1)S(1)} all-to-all(bf16[16,32,2048]{2,1,0:T(8,128)(2,1)S(1)} %bitcast.66), channel_id=1, replica_groups=mesh['vp'=16,'op'=8] {'vp'}, dimensions={0} | all-to-all | bytes 4194304 | tf_op jit(solution)/shard_map/all_to_all | solution.py:37
  217.2 9.1 %fusion.11 = bf16[512,2048]{1,0:T(8,128)(2,1)} fusion(bf16[512,2048]{1,0:T(8,128)(2,1)S(1)} %bitcast.61, bf16[1,2048,2048]{2,1,0:T(8,128)(2,1)} %param.4), kind=kOutput, calls=%fused_computation.17 | convolution fusion | flops 4296015872 | bytes 12582912 | tf_op jit(solution)/shard_map/dot_general | solution.py:40
  226.4 3.5 %all-to-all-start.9 = ((bf16[16,32,256]{2,1,0:T(8,128)(2,1)}), bf16[16,32,256]{2,1,0:T(8,128)(2,1)S(1)}, u32[]{:S(2)}, u32[]{:S(2)}) async-start(bf16[16,32,256]{2,1,0:T(8,128)(2,1)} %bitcast.72), calls=%async_computation.14 | async-start | bytes 524288 | tf_op jit(solution)/shard_map/all_to_all | solution.py:44
  230.0 8.6 %all-to-all-done.9 = bf16[16,32,256]{2,1,0:T(8,128)(2,1)S(1)} async-done(((bf16[16,32,256]{2,1,0:T(8,128)(2,1)}), bf16[16,32,256]{2,1,0:T(8,128)(2,1)S(1)}, u32[]{:S(2)}, u32[]{:S(2)}) %all-to-all-start.9) | async-done | bytes 262176 | tf_op jit(solution)/shard_map/all_to_all | solution.py:44
  238.6 3.5 %all-to-all-start.3 = ((bf16[16,32,256]{2,1,0:T(8,128)(2,1)}), bf16[16,32,256]{2,1,0:T(8,128)(2,1)S(1)}, u32[]{:S(2)}, u32[]{:S(2)}) async-start(bf16[16,32,256]{2,1,0:T(8,128)(2,1)} %bitcast.71), calls=%async_computation.5 | async-start | bytes 524288 | tf_op jit(solution)/shard_map/all_to_all | solution.py:44
  242.7 8.1 %all-to-all-done.3 = bf16[16,32,256]{2,1,0:T(8,128)(2,1)S(1)} async-done(((bf16[16,32,256]{2,1,0:T(8,128)(2,1)}), bf16[16,32,256]{2,1,0:T(8,128)(2,1)S(1)}, u32[]{:S(2)}, u32[]{:S(2)}) %all-to-all-start.3) | async-done | bytes 262176 | tf_op jit(solution)/shard_map/all_to_all | solution.py:44
  250.8 3.8 %all-to-all-start.7 = ((bf16[16,32,256]{2,1,0:T(8,128)(2,1)}), bf16[16,32,256]{2,1,0:T(8,128)(2,1)S(1)}, u32[]{:S(2)}, u32[]{:S(2)}) async-start(bf16[16,32,256]{2,1,0:T(8,128)(2,1)} %bitcast.69), calls=%async_computation.11 | async-start | bytes 524288 | tf_op jit(solution)/shard_map/all_to_all | solution.py:44
  255.1 8.0 %all-to-all-done.7 = bf16[16,32,256]{2,1,0:T(8,128)(2,1)S(1)} async-done(((bf16[16,32,256]{2,1,0:T(8,128)(2,1)}), bf16[16,32,256]{2,1,0:T(8,128)(2,1)S(1)}, u32[]{:S(2)}, u32[]{:S(2)}) %all-to-all-start.7) | async-done | bytes 262176 | tf_op jit(solution)/shard_map/all_to_all | solution.py:44
  263.2 4.2 %all-to-all-start.5 = ((bf16[16,32,256]{2,1,0:T(8,128)(2,1)}), bf16[16,32,256]{2,1,0:T(8,128)(2,1)}, u32[]{:S(2)}, u32[]{:S(2)}) async-start(bf16[16,32,256]{2,1,0:T(8,128)(2,1)} %bitcast.68), calls=%async_computation.8 | async-start | bytes 524288 | tf_op jit(solution)/shard_map/all_to_all | solution.py:44
  267.9 8.1 %all-to-all-done.5 = bf16[16,32,256]{2,1,0:T(8,128)(2,1)} async-done(((bf16[16,32,256]{2,1,0:T(8,128)(2,1)}), bf16[16,32,256]{2,1,0:T(8,128)(2,1)}, u32[]{:S(2)}, u32[]{:S(2)}) %all-to-all-start.5) | async-done | bytes 262176 | tf_op jit(solution)/shard_map/all_to_all | solution.py:44
  282.1 6.2 %all-to-all-done.1 = bf16[16,32,256]{2,1,0:T(8,128)(2,1)S(1)} async-done(((bf16[16,32,256]{2,1,0:T(8,128)(2,1)}), bf16[16,32,256]{2,1,0:T(8,128)(2,1)S(1)}, u32[]{:S(2)}, u32[]{:S(2)}) %all-to-all-start.1) | async-done | bytes 262176 | tf_op jit(solution)/shard_map/all_to_all | solution.py:44
  (28 shorter events, 12.5 us)
Async XLA Ops:
  6.5 219.9 %reduce-scatter.14.cloned.1.call-start = ((), (), s32[]{:S(2)}) async-start(), calls=%async_computation.19 | async-start | bytes 2359296 | tf_op jit(solution)/shard_map/reduce_scatter | solution.py:43
  6.5 43.0 %slice-start = ((s8[8388608]{0:T(1024)(128)(4,1)}), s8[4194304]{0:T(1024)(128)(4,1)S(1)}, s32[]{:S(2)}) async-start(s8[8388608]{0:T(1024)(128)(4,1)} %bitcast.78), calls=%async_computation.20 | async-start | bytes 8388608
  8.5 41.0 %slice-start.1 = ((s8[8388608]{0:T(1024)(128)(4,1)}), s8[4194304]{0:T(1024)(128)(4,1)S(1)}, s32[]{:S(2)}) async-start(s8[8388608]{0:T(1024)(128)(4,1)} %bitcast.78), calls=%async_computation.21 | async-start | bytes 8388608
  55.3 174.7 %reduce-scatter.8.cloned.1.call-start = ((), (), s32[]{:S(2)}) async-start(), calls=%async_computation.16 | async-start | bytes 2359296 | tf_op jit(solution)/shard_map/reduce_scatter | solution.py:43
  99.7 143.0 %reduce-scatter.12.cloned.1.call-start = ((), (), s32[]{:S(2)}) async-start(), calls=%async_computation.18 | async-start | bytes 2359296 | tf_op jit(solution)/shard_map/reduce_scatter | solution.py:43
  142.9 112.2 %reduce-scatter.10.cloned.1.call-start = ((), (), s32[]{:S(2)}) async-start(), calls=%async_computation.17 | async-start | bytes 2359296 | tf_op jit(solution)/shard_map/reduce_scatter | solution.py:43
  184.8 83.1 %reduce-scatter.6.cloned.1.call-start = ((), (), s32[]{:S(2)}) async-start(), calls=%async_computation.15 | async-start | bytes 2359296 | tf_op jit(solution)/shard_map/reduce_scatter | solution.py:43
  226.4 12.2 %all-to-all-start.9 = ((bf16[16,32,256]{2,1,0:T(8,128)(2,1)}), bf16[16,32,256]{2,1,0:T(8,128)(2,1)S(1)}, u32[]{:S(2)}, u32[]{:S(2)}) async-start(bf16[16,32,256]{2,1,0:T(8,128)(2,1)} %bitcast.72), calls=%async_computation.14 | async-start | bytes 524288 | tf_op jit(solution)/shard_map/all_to_all | solution.py:44
  238.6 12.2 %all-to-all-start.3 = ((bf16[16,32,256]{2,1,0:T(8,128)(2,1)}), bf16[16,32,256]{2,1,0:T(8,128)(2,1)S(1)}, u32[]{:S(2)}, u32[]{:S(2)}) async-start(bf16[16,32,256]{2,1,0:T(8,128)(2,1)} %bitcast.71), calls=%async_computation.5 | async-start | bytes 524288 | tf_op jit(solution)/shard_map/all_to_all | solution.py:44
  250.8 12.3 %all-to-all-start.7 = ((bf16[16,32,256]{2,1,0:T(8,128)(2,1)}), bf16[16,32,256]{2,1,0:T(8,128)(2,1)S(1)}, u32[]{:S(2)}, u32[]{:S(2)}) async-start(bf16[16,32,256]{2,1,0:T(8,128)(2,1)} %bitcast.69), calls=%async_computation.11 | async-start | bytes 524288 | tf_op jit(solution)/shard_map/all_to_all | solution.py:44
  263.2 12.9 %all-to-all-start.5 = ((bf16[16,32,256]{2,1,0:T(8,128)(2,1)}), bf16[16,32,256]{2,1,0:T(8,128)(2,1)}, u32[]{:S(2)}, u32[]{:S(2)}) async-start(bf16[16,32,256]{2,1,0:T(8,128)(2,1)} %bitcast.68), calls=%async_computation.8 | async-start | bytes 524288 | tf_op jit(solution)/shard_map/all_to_all | solution.py:44
  276.1 12.2 %all-to-all-start.1 = ((bf16[16,32,256]{2,1,0:T(8,128)(2,1)}), bf16[16,32,256]{2,1,0:T(8,128)(2,1)S(1)}, u32[]{:S(2)}, u32[]{:S(2)}) async-start(bf16[16,32,256]{2,1,0:T(8,128)(2,1)} %bitcast.70), calls=%async_computation.2 | async-start | bytes 524288 | tf_op jit(solution)/shard_map/all_to_all | solution.py:44
Sparse Core Ops, SparseCore 0:
  55.4 31.4 reduce-scatter.13
  99.8 31.4 reduce-scatter.7
  143.0 31.3 reduce-scatter.11
  185.0 31.1 reduce-scatter.9
  226.5 30.8 reduce-scatter.5

commit v2 on v1

v2 whole, which is shorter than its diff:
```python
import functools

import jax
import jax.numpy as jnp
import numpy as np
from jax import lax
from jax.experimental import pallas as pl
from jax.experimental.pallas import tpu as pltpu
from jax.sharding import PartitionSpec as P

SIDE = 4
CORES = 2
STEPS = (
    ((0, 0), (0, 0)),
    ((0, 1), (1, 0)),
    ((0, 3), (3, 0)),
    ((1, 0), (0, 1)),
    ((3, 0), (0, 3)),
    ((1, 1), (3, 3)),
    ((3, 3), (1, 1)),
    ((1, 3), (3, 1)),
    ((3, 1), (1, 3)),
    ((0, 2), (2, 0)),
    ((2, 0), (0, 2)),
    ((2, 2), (2, 2)),
    ((1, 2), (2, 1)),
    ((2, 1), (1, 2)),
    ((3, 2), (2, 3)),
    ((2, 3), (3, 2)),
)
GROUPS = (9, 5, 2)
PERMUTED = (2,)
FLIGHT = 4
WAITS = {13: 0}
PLACED = (2, 2, 4, 3, 4)
FLOPS = 1 << 20


PLACES = [
    [[ways[0] for ways in STEPS].index(own[core]) for own in STEPS] for core in range(CORES)
]


def pairs(step, n_op, backward=False):
    made = []
    for vp in range(SIDE * SIDE):
        for op in range(n_op):
            dz, dy = STEPS[step][op % CORES]
            to = ((vp // SIDE + dz) % SIDE) * SIDE + (vp % SIDE + dy) % SIDE
            made.append((vp * n_op + op, to * n_op + op))
    return [(b, a) for a, b in made] if backward else made


def row_slots(classes, capacity):
    rows = classes.shape[1]
    n_step = len(STEPS)
    vp = lax.axis_index("vp")
    table = jnp.asarray(np.array(STEPS, np.int32).transpose(1, 2, 0)[..., None])
    way = jnp.where(lax.axis_index("op") % CORES == 0, table[0], table[1])
    named = (vp // SIDE + way[0]) % SIDE * SIDE + (vp % SIDE + way[1]) % SIDE
    onehot = (classes == named).astype(jnp.bfloat16)
    upto = (
        lax.broadcasted_iota(jnp.int32, (rows, rows), 0)
        <= lax.broadcasted_iota(jnp.int32, (rows, rows), 1)
    ).astype(jnp.bfloat16)
    before = jnp.dot(onehot, upto, preferred_element_type=jnp.float32)
    base = lax.broadcasted_iota(jnp.int32, (n_step, rows), 0) * capacity
    slot = jnp.where(onehot > 0, before.astype(jnp.int32) - 1 + base, 0)
    return jnp.sum(slot, axis=0, keepdims=True)


def tick_body(n_after, _, arrived, w, *refs):
    out = refs[n_after]
    out[...] = jnp.dot(
        arrived[...], w[...], preferred_element_type=jnp.float32
    ).astype(out.dtype)


def tick(arrived, w, held, place, rows, later, after):
    capacity, depth = arrived.shape
    columns = w.shape[1]
    tile = 1024
    whole = pl.BlockSpec(memory_space=pl.ANY)
    extra = [x for x in (held, later) if x is not None]
    out_specs = [pl.BlockSpec((capacity, tile), lambda i, place: (place[0], i))]
    out_shape = [jax.ShapeDtypeStruct((rows * capacity, columns), jnp.bfloat16)]
    aliases = {3: 0} if held is not None else {}
    if later is not None:
        aliases[2 + len(extra)] = 1
        out_specs.append(whole)
        out_shape.append(jax.ShapeDtypeStruct(later.shape, later.dtype))
    extra += after
    return pl.pallas_call(
        functools.partial(tick_body, len(extra)),
        grid_spec=pltpu.PrefetchScalarGridSpec(
            num_scalar_prefetch=1,
            grid=(columns // tile,),
            in_specs=[
                pl.BlockSpec((capacity, depth), lambda i, place: (0, 0)),
                pl.BlockSpec((depth, tile), lambda i, place: (0, i)),
            ] + [whole] * len(extra),
            out_specs=out_specs,
        ),
        out_shape=out_shape,
        input_output_aliases=aliases,
        compiler_params=pltpu.CompilerParams(vmem_limit_bytes=40 << 20),
        cost_estimate=pl.CostEstimate(flops=FLOPS, bytes_accessed=1 << 16, transcendentals=0),
    )(place, arrived, w, *extra)


def place_kernel(first, capacity, slot, amplitudes, *outs):
    for k, out in enumerate(outs):
        wanted = lax.broadcasted_iota(jnp.int32, (capacity, slot.shape[1]), 0) + (first + k) * capacity
        out[...] = jnp.dot(
            (slot[...] == wanted).astype(jnp.float32).astype(jnp.bfloat16), amplitudes[...],
            preferred_element_type=jnp.float32,
        ).astype(out.dtype)


def place(slot, amplitudes, first, count, capacity):
    rows, depth = amplitudes.shape
    tile = 1024
    return pl.pallas_call(
        functools.partial(place_kernel, first, capacity),
        grid=(depth // tile,),
        in_specs=[
            pl.BlockSpec(slot.shape, lambda i: (0, 0)),
            pl.BlockSpec((rows, tile), lambda i: (0, i)),
        ],
        out_specs=[pl.BlockSpec((capacity, tile), lambda i: (0, i))] * count,
        out_shape=[jax.ShapeDtypeStruct((capacity, depth), jnp.bfloat16)] * count,
        compiler_params=pltpu.CompilerParams(vmem_limit_bytes=40 << 20),
        cost_estimate=pl.CostEstimate(flops=FLOPS, bytes_accessed=1 << 16, transcendentals=0),
    )(slot, amplitudes)


def op_pairs(n_op, turn):
    made = []
    for vp in range(SIDE * SIDE):
        for op in range(n_op):
            x, core = turn(op // CORES, op % CORES)
            made.append((vp * n_op + op, vp * n_op + x % (n_op // CORES) * CORES + core))
    return made


def sum_over_op(partial, axes, n_op):
    n_x = n_op // CORES
    me = lax.axis_index("op")
    x, core = me // CORES, me % CORES
    width = partial.shape[1] // n_op
    blocks = [partial[:, b * width : (b + 1) * width] for b in range(n_op)]
    even, odd = (jnp.concatenate(blocks[c::CORES], axis=1) for c in range(CORES))
    other = lax.ppermute(
        jnp.where(core == 0, odd, even), axes, op_pairs(n_op, lambda x, c: (x, 1 - c))
    )
    both = jnp.where(core == 0, even, odd).astype(jnp.float32) + other.astype(jnp.float32)
    both = both.astype(jnp.bfloat16)

    def block(d):
        return lax.dynamic_slice_in_dim(both, (x + d) % n_x * width, width, axis=1)

    terms = [block(0)] + [
        lax.ppermute(block(d), axes, op_pairs(n_op, lambda x, c, d=d: (x + d, c)))
        for d in range(1, n_x)
    ]
    return sum(t.astype(jnp.float32) for t in terms).astype(jnp.bfloat16)


def move_kernel(capacity, order, x, out):
    for i in range(len(STEPS)):
        start = pl.multiple_of(order[i] * capacity, capacity)
        out[i * capacity : (i + 1) * capacity] = x[pl.ds(start, capacity)]


def by_owner(x, capacity):
    vp = lax.axis_index("vp")
    owner = np.arange(SIDE * SIDE)
    step_of = np.zeros((SIDE, SIDE), np.int32)
    for step, ways in enumerate(STEPS):
        step_of[ways[0]] = step
    table = np.stack([
        step_of[(me // SIDE - owner // SIDE) % SIDE, (me % SIDE - owner % SIDE) % SIDE]
        for me in range(SIDE * SIDE)
    ])
    order = lax.dynamic_slice(jnp.asarray(table), (vp, 0), (1, SIDE * SIDE)).reshape(-1)
    return pl.pallas_call(
        functools.partial(move_kernel, capacity),
        in_specs=[pl.BlockSpec(memory_space=pltpu.SMEM), pl.BlockSpec(memory_space=pltpu.VMEM)],
        out_specs=pl.BlockSpec(memory_space=pltpu.VMEM),
        out_shape=jax.ShapeDtypeStruct(x.shape, x.dtype),
    )(order, x)


def local(amplitudes, integrals, pair_class):
    axes = ("vp", "op")
    n_op = lax.axis_size("op")
    rows, depth = amplitudes.shape
    capacity = rows * 5 // 32
    w = integrals[0]
    classes = pair_class.reshape(1, rows)
    slot = row_slots(classes, capacity)

    def send(x, k):
        return lax.ppermute(x, axes, pairs(k, n_op))

    sent = [None]
    for count in PLACED:
        sent += place(slot, amplitudes, len(sent), count, capacity)
    arrived = list(place(slot, amplitudes, 0, 1, capacity))
    arrived += [send(sent[k], k) for k in range(1, 1 + FLIGHT)]
    summed, groups = [], []
    even = lax.axis_index("op") % CORES == 0
    step = 0
    for g, count in enumerate(GROUPS):
        held, first = None, step
        for row in range(count):
            after = groups[-1:] if row == 0 else []
            if step in WAITS:
                after = after + [summed[WAITS[step]]]
            later = step + FLIGHT
            place_now = jnp.where(even, PLACES[0][step] - first, PLACES[1][step] - first)
            place_now = place_now.astype(jnp.int32).reshape(1)
            if step == 0 or later >= len(STEPS):
                [held] = tick(arrived[step], w, held, place_now, count, None, after)
            else:
                held, sent[later] = tick(arrived[step], w, held, place_now, count, sent[later], after)
                arrived.append(send(sent[later], later))
            step += 1
        groups.append(held)
        if g in PERMUTED:
            summed.append(sum_over_op(held, axes, n_op))
        else:
            summed.append(lax.psum_scatter(held, "op", scatter_dimension=1, tiled=True))
    back = lax.all_to_all(
        by_owner(jnp.concatenate(summed, axis=0), capacity), "vp", split_axis=0, concat_axis=0, tiled=True
    )
    home = classes * capacity + slot % capacity
    wanted = lax.broadcasted_iota(jnp.int32, (back.shape[0], rows), 0)
    return lax.dot_general(
        back, (home == wanted).astype(jnp.bfloat16), (((0,), (0,)), ((), ())),
        preferred_element_type=jnp.float32,
    ).astype(jnp.bfloat16)


def solution(mesh):
    return jax.shard_map(
        local,
        mesh=mesh,
        in_specs=(P("vp", "op"), P("vp", "op", None), P("vp", None)),
        out_specs=P("op", "vp"),
        check_vma=False,
    )
```

time: 298 us -> 263 us (0.88)
  blocking collectives: 152 us -> 0 us
  Pallas kernels: 0 us -> 85.3 us
  matrix products: 72.9 us -> 3.83 us
  waiting for transfers between devices: 39.2 us -> 78.5 us
  starting transfers between devices: 18.7 us -> 48.8 us
  local copies, waits for them, and re-layouts: 0.01 us -> 28.2 us
    all_to_all x5 -> x0, blocking collectives: 152 us -> none  [local(): lax.all_to_all(sent.reshape(n_class, size, depth), 'vp', split_axis=0, co...]
    pallas_call x0 -> x23, Pallas kernels: none -> 85.3 us  [the longest x16 64.7 us: tick(): pl.pallas_call(functools.partial(tick_body, len(extra)), grid_spec=pltpu....]
    dot_general x16 -> x2, matrix products: 72.9 us -> 3.83 us  [the longest x1 2.67 us: local(): lax.dot_general(back, (home == wanted).astype(jnp.bfloat16), (((0,), (0,)...]
    ppermute x0 -> x19, waiting for transfers between devices: none -> 57.9 us  [the longest x15 50.8 us: send(): return lax.ppermute(x, axes, pairs(k, n_op))]
    ppermute x0 -> x19, starting transfers between devices: none -> 37.1 us  [the longest x15 31.4 us: send(): return lax.ppermute(x, axes, pairs(k, n_op))]
    unnamed x4 -> x30, local copies, waits for them, and re-layouts: 0.01 us -> 26.8 us
    all_to_all x5 -> x1, waiting for transfers between devices: 39.1 us -> 20.5 us  [local(): lax.all_to_all(by_owner(jnp.concatenate(summed, axis=0), capacity), 'vp',...]
    all_to_all x5 -> x1, starting transfers between devices: 18.5 us -> 11.6 us  [local(): lax.all_to_all(by_owner(jnp.concatenate(summed, axis=0), capacity), 'vp',...]
  transfers between devices with their start and end apart: 10 -> 22, of which waited for: 5 -> 9; matrix products, arithmetic and copies ran while one was open for 20% -> 1% of each run, Pallas kernels for 0% -> 27%
where the time goes in v2:
time: 263 us; the launch traced here: 262 us
  Pallas kernels  85.3 us (32%)
  waiting for transfers between devices  78.5 us (30%)
  starting transfers between devices  48.8 us (19%)
  local copies, waits for them, and re-layouts  28.2 us (11%)
  between operations  13.8 us (5%)
  matrix products  3.83 us (1%)
  other arithmetic  3.4 us (1%)
    pallas_call x16, Pallas kernels, tick(): pl.pallas_call(functools.partial(tick_body, len(extra)), grid_spec=pltpu....  64.7 us
    ppermute x15, waiting for transfers between devices, send(): return lax.ppermute(x, axes, pairs(k, n_op))  50.8 us
    ppermute x15, starting transfers between devices, send(): return lax.ppermute(x, axes, pairs(k, n_op))  31.4 us
    unnamed x30, local copies, waits for them, and re-layouts  26.8 us
    all_to_all x1, waiting for transfers between devices, local(): lax.all_to_all(by_owner(jnp.concatenate(summed, axis=0), capacity), 'vp',...  20.5 us
    pallas_call x6, Pallas kernels, place(): pl.pallas_call(functools.partial(place_kernel, first, capacity), grid=(de...  18.2 us
    all_to_all x1, starting transfers between devices, local(): lax.all_to_all(by_owner(jnp.concatenate(summed, axis=0), capacity), 'vp',...  11.6 us
    ppermute x3, starting transfers between devices, sum_over_op(): lax.ppermute(block(d), axes, op_pairs(n_op, lambda x, c, d=d: (x + d, c)))  5.7 us
  transfers between devices with their start and end apart: 22, of which 9 were waited for; matrix products, arithmetic and copies ran while one was open for 1% of the time, Pallas kernels for 27%

profile of v2, /device:TPU:0, one launch (start us, length us, event | category | flops | bytes accessed | tf_op | source)
XLA Modules:
  0.0 261.8 jit_solution(16038841835661105660)
XLA Ops:
  26.9 4.4 %shard_map.59 = (bf16[160,2048]{1,0:T(8,128)(2,1)}, bf16[160,2048]{1,0:T(8,128)(2,1)}, bf16[160,2048]{1,0:T(8,128)(2,1)}, bf16[160,2048]{1,0:T(8,128)(2,1)}) custom-call(s32[1,1024]{1,0:T(1,128)S(1)} %bitcast.47, bf16[1024,2048]{1,0:T(8,128)(2,1)S(1)} %copy-done.8), custom_call_target="tpu_custom_call" | custom-call | flops 1048576 | bytes 65536 | tf_op jit(solution)/shard_map/pallas_call | solution.py:123
  31.3 4.4 %shard_map.58.refs_0_ = bf16[1440,2048]{1,0:T(8,128)(2,1)S(1)} custom-call(s32[1]{0:T(128)} %constant.121.clone.1._, bf16[160,2048]{1,0:T(8,128)(2,1)S(1)} %shard_map.57.arrived, bf16[2048,2048]{1,0:T(8,128)(2,1)} %bitcast.28), custom_call_target="tpu_custom_call" | custom-call | flops 1048576 | bytes 65536 | tf_op jit(solution)/shard_map/pallas_call | solution.py:93
  35.7 4.4 %shard_map.60 = (bf16[1440,2048]{1,0:T(8,128)(2,1)S(1)}, bf16[160,2048]{1,0:T(8,128)(2,1)}) custom-call(s32[1]{0:T(128)} %bitcast.10._, bf16[160,2048]{1,0:T(8,128)(2,1)S(1)} %collective-permute-done.3.arrived, bf16[2048,2048]{1,0:T(8,128)(2,1)} %bitcast.29, bf16[1440,2048]{1,0:T(8,128)(2,1)S(1)} %shard_map.58.refs_0_, ...), custom_call_target="tpu_custom_call", output_to_operand_aliasing={{0}: (3, {}), {1}: (4, {})} | custom-call | flops 1048576 | bytes 65536 | tf_op jit(solution)/shard_map/pallas_call | solution.py:93
  40.2 4.4 %shard_map.61 = (bf16[1440,2048]{1,0:T(8,128)(2,1)S(1)}, bf16[160,2048]{1,0:T(8,128)(2,1)}) custom-call(s32[1]{0:T(128)} %bitcast.9._, bf16[160,2048]{1,0:T(8,128)(2,1)S(1)} %collective-permute-done.2.arrived, bf16[2048,2048]{1,0:T(8,128)(2,1)} %bitcast.30, ...), custom_call_target="tpu_custom_call", output_to_operand_aliasing={{0}: (3, {}), {1}: (4, {})} | custom-call | flops 1048576 | bytes 65536 | tf_op jit(solution)/shard_map/pallas_call | solution.py:93
  44.6 5.4 %collective-permute-start.6 = (bf16[160,2048]{1,0:T(8,128)(2,1)}, bf16[160,2048]{1,0:T(8,128)(2,1)S(1)}, u32[]{:S(2)}, u32[]{:S(2)}) collective-permute-start(bf16[160,2048]{1,0:T(8,128)(2,1)} %get-tuple-element.55), channel_id=1, source_target_pairs={{0,120},{1,41},{2,122},{3,43},{4,124},{5,45},{6,126},{7,47},{8,96}... | collective-permute-start | bytes 1966088 | tf_op jit(solution)/shard_map/ppermute | solution.py:204
  50.0 4.4 %shard_map.62 = (bf16[1440,2048]{1,0:T(8,128)(2,1)S(1)}, bf16[160,2048]{1,0:T(8,128)(2,1)}) custom-call(s32[1]{0:T(128)} %bitcast.8._, bf16[160,2048]{1,0:T(8,128)(2,1)S(1)} %collective-permute-done.1.arrived, bf16[2048,2048]{1,0:T(8,128)(2,1)} %bitcast.31, ...), custom_call_target="tpu_custom_call", output_to_operand_aliasing={{0}: (3, {}), {1}: (4, {})} | custom-call | flops 1048576 | bytes 65536 | tf_op jit(solution)/shard_map/pallas_call | solution.py:93
  54.4 4.4 %shard_map.63 = (bf16[1440,2048]{1,0:T(8,128)(2,1)S(1)}, bf16[160,2048]{1,0:T(8,128)(2,1)}) custom-call(s32[1]{0:T(128)} %bitcast.2._, bf16[160,2048]{1,0:T(8,128)(2,1)S(1)} %collective-permute-done.arrived, bf16[2048,2048]{1,0:T(8,128)(2,1)} %bitcast.32, ...), custom_call_target="tpu_custom_call", output_to_operand_aliasing={{0}: (3, {}), {1}: (4, {})} | custom-call | flops 1048576 | bytes 65536 | tf_op jit(solution)/shard_map/pallas_call | solution.py:93
  61.4 4.1 %collective-permute-start.4 = (bf16[160,2048]{1,0:T(8,128)(2,1)}, bf16[160,2048]{1,0:T(8,128)(2,1)}, u32[]{:S(2)}, u32[]{:S(2)}) collective-permute-start(bf16[160,2048]{1,0:T(8,128)(2,1)} %get-tuple-element.53), channel_id=1, source_target_pairs={{0,104},{1,57},{2,106},{3,59},{4,108},{5,61},{6,110},{7,63},{8,112... | collective-permute-start | bytes 1966088 | tf_op jit(solution)/shard_map/ppermute | solution.py:204
  74.7 4.4 %shard_map.65 = (bf16[1440,2048]{1,0:T(8,128)(2,1)S(1)}, bf16[160,2048]{1,0:T(8,128)(2,1)}) custom-call(s32[1]{0:T(128)} %bitcast.13._, bf16[160,2048]{1,0:T(8,128)(2,1)S(1)} %collective-permute-done.7.arrived, bf16[2048,2048]{1,0:T(8,128)(2,1)} %bitcast.33, bf16[1440,2048]{1,0:T(8,128)(2,1)S(1)} %copy-done.4, ...), custom_call_target="tpu_custom_call", output_to_operand_aliasing={{0}: (3, {}), {1}: (4, {})} | custom-call | flops 1048576 | bytes 65536 | tf_op jit(solution)/shard_map/pallas_call | solution.py:93
  79.1 4.4 %shard_map.66 = (bf16[1440,2048]{1,0:T(8,128)(2,1)S(1)}, bf16[160,2048]{1,0:T(8,128)(2,1)}) custom-call(s32[1]{0:T(128)} %bitcast.12._, bf16[160,2048]{1,0:T(8,128)(2,1)S(1)} %collective-permute-done.6.arrived, bf16[2048,2048]{1,0:T(8,128)(2,1)} %bitcast.34, ...), custom_call_target="tpu_custom_call", output_to_operand_aliasing={{0}: (3, {}), {1}: (4, {})} | custom-call | flops 1048576 | bytes 65536 | tf_op jit(solution)/shard_map/pallas_call | solution.py:93
  83.5 4.6 %shard_map.67 = (bf16[1440,2048]{1,0:T(8,128)(2,1)S(1)}, bf16[160,2048]{1,0:T(8,128)(2,1)}) custom-call(s32[1]{0:T(128)} %bitcast.11._, bf16[160,2048]{1,0:T(8,128)(2,1)} %collective-permute-done.5.arrived, bf16[2048,2048]{1,0:T(8,128)(2,1)} %bitcast.35, ...), custom_call_target="tpu_custom_call", output_to_operand_aliasing={{0}: (3, {}), {1}: (4, {})} | custom-call | flops 1048576 | bytes 65536 | tf_op jit(solution)/shard_map/pallas_call | solution.py:93
  88.1 4.6 %shard_map.69 = (bf16[1440,2048]{1,0:T(8,128)(2,1)S(1)}, bf16[160,2048]{1,0:T(8,128)(2,1)S(1)}) custom-call(s32[1]{0:T(128)} %bitcast.1._, bf16[160,2048]{1,0:T(8,128)(2,1)} %collective-permute-done.4.arrived, bf16[2048,2048]{1,0:T(8,128)(2,1)} %bitcast.36, ...), custom_call_target="tpu_custom_call", output_to_operand_aliasing={{0}: (3, {}), {1}: (4, {})} | custom-call | flops 1048576 | bytes 65536 | tf_op jit(solution)/shard_map/pallas_call | solution.py:93
  97.0 5.7 %collective-permute-start.11 = (bf16[160,2048]{1,0:T(8,128)(2,1)}, bf16[160,2048]{1,0:T(8,128)(2,1)}, u32[]{:S(2)}, u32[]{:S(2)}) collective-permute-start(bf16[160,2048]{1,0:T(8,128)(2,1)} %get-tuple-element.70), channel_id=1, source_target_pairs={{0,80},{1,81},{2,82},{3,83},{4,84},{5,85},{6,86},{7,87},{8,88},{9,... | collective-permute-start | bytes 1966088 | tf_op jit(solution)/shard_map/ppermute | solution.py:204
  102.7 13.1 %collective-permute-done.8.arrived = bf16[160,2048]{1,0:T(8,128)(2,1)} collective-permute-done((bf16[160,2048]{1,0:T(8,128)(2,1)}, bf16[160,2048]{1,0:T(8,128)(2,1)}, u32[]{:S(2)}, u32[]{:S(2)}) %collective-permute-start.8) | collective-permute-done | bytes 655392 | tf_op jit(solution)/shard_map/ppermute | solution.py:204
  118.6 5.5 %shard_map.70 = (bf16[800,2048]{1,0:T(8,128)(2,1)}, bf16[160,2048]{1,0:T(8,128)(2,1)S(1)}) custom-call(s32[1]{0:T(128)} %bitcast.15._, bf16[160,2048]{1,0:T(8,128)(2,1)} %collective-permute-done.8.arrived, bf16[2048,2048]{1,0:T(8,128)(2,1)} %bitcast.37, bf16[160,2048]{1,0:T(8,128)(2,1)S(1)} %get-tuple-element.67.refs_0_, ...), custom_call_target="tpu_custom_call", output_to_operand_aliasing={{1}: (3, {})} | custom-call | flops 1048576 | bytes 65536 | tf_op jit(solution)/shard_map/pallas_call | solution.py:93
  131.5 3.9 %shard_map.72 = (bf16[800,2048]{1,0:T(8,128)(2,1)}, bf16[160,2048]{1,0:T(8,128)(2,1)S(1)}) custom-call(s32[1]{0:T(128)} %constant.124.clone.1._, bf16[160,2048]{1,0:T(8,128)(2,1)} %collective-permute-done.11.arrived, bf16[2048,2048]{1,0:T(8,128)(2,1)S(1)} %bitcast.39, ...), custom_call_target="tpu_custom_call", output_to_operand_aliasing={{0}: (3, {}), {1}: (4, {})} | custom-call | flops 1048576 | bytes 65536 | tf_op jit(solution)/shard_map/pallas_call | solution.py:93
  135.4 9.6 %collective-permute-done.10.arrived = bf16[160,2048]{1,0:T(8,128)(2,1)S(1)} collective-permute-done((bf16[160,2048]{1,0:T(8,128)(2,1)S(1)}, bf16[160,2048]{1,0:T(8,128)(2,1)S(1)}, u32[]{:S(2)}, u32[]{:S(2)}) %collective-permute-start.10) | collective-permute-done | bytes 655392 | tf_op jit(solution)/shard_map/ppermute | solution.py:204
  148.0 7.7 %collective-permute-done.9.arrived = bf16[160,2048]{1,0:T(8,128)(2,1)} collective-permute-done((bf16[160,2048]{1,0:T(8,128)(2,1)S(1)}, bf16[160,2048]{1,0:T(8,128)(2,1)}, u32[]{:S(2)}, u32[]{:S(2)}) %collective-permute-start.9) | collective-permute-done | bytes 655392 | tf_op jit(solution)/shard_map/ppermute | solution.py:204
  160.3 3.9 %shard_map.74.refs_0_ = bf16[800,2048]{1,0:T(8,128)(2,1)} custom-call(s32[1]{0:T(128)} %bitcast.14._, bf16[160,2048]{1,0:T(8,128)(2,1)} %collective-permute-done.9.arrived, bf16[2048,2048]{1,0:T(8,128)(2,1)S(1)} %bitcast.41, bf16[800,2048]{1,0:T(8,128)(2,1)} %shard_map.73.refs_0_, bf16[1440,256]{1,0:T(8,128)(2,1)S(1)} %copy-done.10), custom_call_target="tpu_custom_call", output_to_operand_aliasing={{}: (3, {})} | custom-call | flops 1048576 | bytes 65536 | tf_op jit(solution)/shard_map/pallas_call | solution.py:93
  166.9 5.1 %collective-permute-start.13 = (bf16[160,2048]{1,0:T(8,128)(2,1)S(1)}, bf16[160,2048]{1,0:T(8,128)(2,1)S(1)}, u32[]{:S(2)}, u32[]{:S(2)}) collective-permute-start(bf16[160,2048]{1,0:T(8,128)(2,1)S(1)} %get-tuple-element.77), channel_id=1, source_target_pairs={{0,88},{1,113},{2,90},{3,115},{4,92},{5,117},{6,94},{7,119},{8,64}... | collective-permute-start | bytes 1966088 | tf_op jit(solution)/shard_map/ppermute | solution.py:204
  171.9 18.5 %collective-permute-done.14.arrived = bf16[160,2048]{1,0:T(8,128)(2,1)S(1)} collective-permute-done((bf16[160,2048]{1,0:T(8,128)(2,1)S(1)}, bf16[160,2048]{1,0:T(8,128)(2,1)S(1)}, u32[]{:S(2)}, u32[]{:S(2)}) %collective-permute-start.14) | collective-permute-done | bytes 655392 | tf_op jit(solution)/shard_map/ppermute | solution.py:204
  210.9 4.5 %collective-permute-done.17 = bf16[320,256]{1,0:T(8,128)(2,1)S(1)} collective-permute-done((bf16[320,256]{1,0:T(8,128)(2,1)S(1)}, bf16[320,256]{1,0:T(8,128)(2,1)S(1)}, u32[]{:S(2)}, u32[]{:S(2)}) %collective-permute-start.17) | collective-permute-done | bytes 163872 | tf_op jit(solution)/shard_map/ppermute | solution.py:163
  220.2 11.6 %all-to-all-start = ((bf16[16,160,256]{2,1,0:T(8,128)(2,1)}), bf16[16,160,256]{2,1,0:T(8,128)(2,1)S(1)}, u32[]{:S(2)}, u32[]{:S(2)}) async-start(bf16[16,160,256]{2,1,0:T(8,128)(2,1)} %bitcast.50), calls=%async_computation.2 | async-start | bytes 2621440 | tf_op jit(solution)/shard_map/all_to_all | solution.py:234
  231.8 20.5 %all-to-all-done = bf16[16,160,256]{2,1,0:T(8,128)(2,1)S(1)} async-done(((bf16[16,160,256]{2,1,0:T(8,128)(2,1)}), bf16[16,160,256]{2,1,0:T(8,128)(2,1)S(1)}, u32[]{:S(2)}, u32[]{:S(2)}) %all-to-all-start) | async-done | bytes 1310752 | tf_op jit(solution)/shard_map/all_to_all | solution.py:234
  (87 shorter events, 84.8 us)
Async XLA Ops:
  6.5 149.2 %reduce-scatter.3.cloned.1.call-start = ((), (), s32[]{:S(2)}) async-start(), calls=%async_computation.3 | async-start | bytes 6635520 | tf_op jit(solution)/shard_map/reduce_scatter | solution.py:233
  13.2 22.5 %collective-permute-start.3 = (bf16[160,2048]{1,0:T(8,128)(2,1)}, bf16[160,2048]{1,0:T(8,128)(2,1)S(1)}, u32[]{:S(2)}, u32[]{:S(2)}) collective-permute-start(bf16[160,2048]{1,0:T(8,128)(2,1)} %get-tuple-element.45), channel_id=1, source_target_pairs={{0,8},{1,33},{2,10},{3,35},{4,12},{5,37},{6,14},{7,39},{8,16},{9,4... | collective-permute-start | bytes 1966088 | tf_op jit(solution)/shard_map/ppermute | solution.py:204
  14.9 25.3 %collective-permute-start.2 = (bf16[160,2048]{1,0:T(8,128)(2,1)S(1)}, bf16[160,2048]{1,0:T(8,128)(2,1)S(1)}, u32[]{:S(2)}, u32[]{:S(2)}) collective-permute-start(bf16[160,2048]{1,0:T(8,128)(2,1)S(1)} %get-tuple-element.44), channel_id=1, source_target_pairs={{0,24},{1,97},{2,26},{3,99},{4,28},{5,101},{6,30},{7,103},{8,0},{9... | collective-permute-start | bytes 1966088 | tf_op jit(solution)/shard_map/ppermute | solution.py:204
  19.2 30.7 %collective-permute-start.1 = (bf16[160,2048]{1,0:T(8,128)(2,1)}, bf16[160,2048]{1,0:T(8,128)(2,1)S(1)}, u32[]{:S(2)}, u32[]{:S(2)}) collective-permute-start(bf16[160,2048]{1,0:T(8,128)(2,1)} %get-tuple-element.43), channel_id=1, source_target_pairs={{0,32},{1,9},{2,34},{3,11},{4,36},{5,13},{6,38},{7,15},{8,40},{9,1... | collective-permute-start | bytes 1966088 | tf_op jit(solution)/shard_map/ppermute | solution.py:204
  21.2 33.2 %collective-permute-start = (bf16[160,2048]{1,0:T(8,128)(2,1)}, bf16[160,2048]{1,0:T(8,128)(2,1)S(1)}, u32[]{:S(2)}, u32[]{:S(2)}) collective-permute-start(bf16[160,2048]{1,0:T(8,128)(2,1)} %get-tuple-element.42), channel_id=1, source_target_pairs={{0,96},{1,25},{2,98},{3,27},{4,100},{5,29},{6,102},{7,31},{8,104},... | collective-permute-start | bytes 1966088 | tf_op jit(solution)/shard_map/ppermute | solution.py:204
  40.1 34.6 %collective-permute-start.7 = (bf16[160,2048]{1,0:T(8,128)(2,1)}, bf16[160,2048]{1,0:T(8,128)(2,1)S(1)}, u32[]{:S(2)}, u32[]{:S(2)}) collective-permute-start(bf16[160,2048]{1,0:T(8,128)(2,1)} %get-tuple-element.56), channel_id=1, source_target_pairs={{0,40},{1,121},{2,42},{3,123},{4,44},{5,125},{6,46},{7,127},{8,48}... | collective-permute-start | bytes 1966088 | tf_op jit(solution)/shard_map/ppermute | solution.py:204
  44.6 34.5 %collective-permute-start.6 = (bf16[160,2048]{1,0:T(8,128)(2,1)}, bf16[160,2048]{1,0:T(8,128)(2,1)S(1)}, u32[]{:S(2)}, u32[]{:S(2)}) collective-permute-start(bf16[160,2048]{1,0:T(8,128)(2,1)} %get-tuple-element.55), channel_id=1, source_target_pairs={{0,120},{1,41},{2,122},{3,43},{4,124},{5,45},{6,126},{7,47},{8,96}... | collective-permute-start | bytes 1966088 | tf_op jit(solution)/shard_map/ppermute | solution.py:204
  54.4 29.2 %collective-permute-start.5 = (bf16[160,2048]{1,0:T(8,128)(2,1)}, bf16[160,2048]{1,0:T(8,128)(2,1)}, u32[]{:S(2)}, u32[]{:S(2)}) collective-permute-start(bf16[160,2048]{1,0:T(8,128)(2,1)} %get-tuple-element.54), channel_id=1, source_target_pairs={{0,56},{1,105},{2,58},{3,107},{4,60},{5,109},{6,62},{7,111},{8,32}... | collective-permute-start | bytes 1966088 | tf_op jit(solution)/shard_map/ppermute | solution.py:204
  61.4 26.7 %collective-permute-start.4 = (bf16[160,2048]{1,0:T(8,128)(2,1)}, bf16[160,2048]{1,0:T(8,128)(2,1)}, u32[]{:S(2)}, u32[]{:S(2)}) collective-permute-start(bf16[160,2048]{1,0:T(8,128)(2,1)} %get-tuple-element.53), channel_id=1, source_target_pairs={{0,104},{1,57},{2,106},{3,59},{4,108},{5,61},{6,110},{7,63},{8,112... | collective-permute-start | bytes 1966088 | tf_op jit(solution)/shard_map/ppermute | solution.py:204
  96.1 119.4 %reduce-scatter.5.cloned.1.call-start = ((), (), s32[]{:S(2)}) async-start(), calls=%async_computation.4 | async-start | bytes 3686400 | tf_op jit(solution)/shard_map/reduce_scatter | solution.py:233
  96.1 19.7 %collective-permute-start.8 = (bf16[160,2048]{1,0:T(8,128)(2,1)}, bf16[160,2048]{1,0:T(8,128)(2,1)}, u32[]{:S(2)}, u32[]{:S(2)}) collective-permute-start(bf16[160,2048]{1,0:T(8,128)(2,1)} %get-tuple-element.66), channel_id=1, source_target_pairs={{0,16},{1,65},{2,18},{3,67},{4,20},{5,69},{6,22},{7,71},{8,24},{9,... | collective-permute-start | bytes 1966088 | tf_op jit(solution)/shard_map/ppermute | solution.py:204
  97.0 27.1 %collective-permute-start.12 = (bf16[160,2048]{1,0:T(8,128)(2,1)}, bf16[160,2048]{1,0:T(8,128)(2,1)}, u32[]{:S(2)}, u32[]{:S(2)}) collective-permute-start(bf16[160,2048]{1,0:T(8,128)(2,1)} %get-tuple-element.71), channel_id=1, source_target_pairs={{0,64},{1,17},{2,66},{3,19},{4,68},{5,21},{6,70},{7,23},{8,72},{9,... | collective-permute-start | bytes 1966088 | tf_op jit(solution)/shard_map/ppermute | solution.py:204
  97.0 34.5 %collective-permute-start.11 = (bf16[160,2048]{1,0:T(8,128)(2,1)}, bf16[160,2048]{1,0:T(8,128)(2,1)}, u32[]{:S(2)}, u32[]{:S(2)}) collective-permute-start(bf16[160,2048]{1,0:T(8,128)(2,1)} %get-tuple-element.70), channel_id=1, source_target_pairs={{0,80},{1,81},{2,82},{3,83},{4,84},{5,85},{6,86},{7,87},{8,88},{9,... | collective-permute-start | bytes 1966088 | tf_op jit(solution)/shard_map/ppermute | solution.py:204
  102.7 42.3 %collective-permute-start.10 = (bf16[160,2048]{1,0:T(8,128)(2,1)S(1)}, bf16[160,2048]{1,0:T(8,128)(2,1)S(1)}, u32[]{:S(2)}, u32[]{:S(2)}) collective-permute-start(bf16[160,2048]{1,0:T(8,128)(2,1)S(1)} %copy-done.13), channel_id=1, source_target_pairs={{0,48},{1,73},{2,50},{3,75},{4,52},{5,77},{6,54},{7,79},{8,56},{9,... | collective-permute-start | bytes 1966088 | tf_op jit(solution)/shard_map/ppermute | solution.py:204
  124.1 31.7 %collective-permute-start.9 = (bf16[160,2048]{1,0:T(8,128)(2,1)S(1)}, bf16[160,2048]{1,0:T(8,128)(2,1)}, u32[]{:S(2)}, u32[]{:S(2)}) collective-permute-start(bf16[160,2048]{1,0:T(8,128)(2,1)S(1)} %get-tuple-element.68), channel_id=1, source_target_pairs={{0,72},{1,49},{2,74},{3,51},{4,76},{5,53},{6,78},{7,55},{8,80},{9,... | collective-permute-start | bytes 1966088 | tf_op jit(solution)/shard_map/ppermute | solution.py:204
  164.1 26.3 %collective-permute-start.14 = (bf16[160,2048]{1,0:T(8,128)(2,1)S(1)}, bf16[160,2048]{1,0:T(8,128)(2,1)S(1)}, u32[]{:S(2)}, u32[]{:S(2)}) collective-permute-start(bf16[160,2048]{1,0:T(8,128)(2,1)S(1)} %get-tuple-element.78), channel_id=1, source_target_pairs={{0,112},{1,89},{2,114},{3,91},{4,116},{5,93},{6,118},{7,95},{8,120... | collective-permute-start | bytes 1966088 | tf_op jit(solution)/shard_map/ppermute | solution.py:204
  166.9 31.3 %collective-permute-start.13 = (bf16[160,2048]{1,0:T(8,128)(2,1)S(1)}, bf16[160,2048]{1,0:T(8,128)(2,1)S(1)}, u32[]{:S(2)}, u32[]{:S(2)}) collective-permute-start(bf16[160,2048]{1,0:T(8,128)(2,1)S(1)} %get-tuple-element.77), channel_id=1, source_target_pairs={{0,88},{1,113},{2,90},{3,115},{4,92},{5,117},{6,94},{7,119},{8,64}... | collective-permute-start | bytes 1966088 | tf_op jit(solution)/shard_map/ppermute | solution.py:204
  200.8 2.2 collective-permute-start.15
  203.3 12.2 %copy-start.11 = (bf16[1440,256]{1,0:T(8,128)(2,1)S(1)}, bf16[1440,256]{1,0:T(8,128)(2,1)}, u32[]{:S(2)}) copy-start(bf16[1440,256]{1,0:T(8,128)(2,1)} %reduce-scatter.3.cloned.1.call-done.refs_1_) | copy-start | bytes 2211844
  203.4 7.5 %collective-permute-start.16 = (bf16[320,256]{1,0:T(8,128)(2,1)S(1)}, bf16[320,256]{1,0:T(8,128)(2,1)S(1)}, u32[]{:S(2)}, u32[]{:S(2)}) collective-permute-start(bf16[320,256]{1,0:T(8,128)(2,1)S(1)} %get-tuple-element.87), channel_id=1, source_target_pairs={{0,2},{1,3},{2,4},{3,5},{4,6},{5,7},{6,0},{7,1},{8,10},{9,11},{10,... | collective-permute-start | bytes 491528 | tf_op jit(solution)/shard_map/ppermute | solution.py:163
  204.9 10.5 %collective-permute-start.17 = (bf16[320,256]{1,0:T(8,128)(2,1)S(1)}, bf16[320,256]{1,0:T(8,128)(2,1)S(1)}, u32[]{:S(2)}, u32[]{:S(2)}) collective-permute-start(bf16[320,256]{1,0:T(8,128)(2,1)S(1)} %get-tuple-element.89), channel_id=1, source_target_pairs={{0,4},{1,5},{2,6},{3,7},{4,0},{5,1},{6,2},{7,3},{8,12},{9,13},{10,... | collective-permute-start | bytes 491528 | tf_op jit(solution)/shard_map/ppermute | solution.py:163
  207.6 7.7 %collective-permute-start.18 = (bf16[320,256]{1,0:T(8,128)(2,1)S(1)}, bf16[320,256]{1,0:T(8,128)(2,1)S(1)}, u32[]{:S(2)}, u32[]{:S(2)}) collective-permute-start(bf16[320,256]{1,0:T(8,128)(2,1)S(1)} %get-tuple-element.88), channel_id=1, source_target_pairs={{0,6},{1,7},{2,0},{3,1},{4,2},{5,3},{6,4},{7,5},{8,14},{9,15},{10,... | collective-permute-start | bytes 491528 | tf_op jit(solution)/shard_map/ppermute | solution.py:163
  220.2 11.6 %copy-start.14 = (s32[1024,1]{0,1:T(1,128)S(1)}, s32[1024,1]{0,1:T(1,128)}, u32[]{:S(2)}) copy-start(s32[1024,1]{0,1:T(1,128)} %param.7) | copy-start | bytes 12292
  220.2 32.1 %all-to-all-start = ((bf16[16,160,256]{2,1,0:T(8,128)(2,1)}), bf16[16,160,256]{2,1,0:T(8,128)(2,1)S(1)}, u32[]{:S(2)}, u32[]{:S(2)}) async-start(bf16[16,160,256]{2,1,0:T(8,128)(2,1)} %bitcast.50), calls=%async_computation.2 | async-start | bytes 2621440 | tf_op jit(solution)/shard_map/all_to_all | solution.py:234
  (13 other events, 40.5 us)
Sparse Core Ops, SparseCore 0:
  96.2 39.6 reduce-scatter.2
  164.3 39.8 reduce-scatter.4

commit v3 on v1

v3 whole, which is shorter than its diff:
```python
import functools

import jax
import jax.numpy as jnp
from jax import lax
from jax.experimental import pallas as pl
from jax.experimental.pallas import tpu as pltpu
from jax.sharding import PartitionSpec as P

CHUNKS = (112, 48)


def row_positions(classes, n_class):
    rows = classes.shape[1]
    named = classes == lax.broadcasted_iota(jnp.int32, (n_class, rows), 0)
    upto = (
        lax.broadcasted_iota(jnp.int32, (rows, rows), 0)
        <= lax.broadcasted_iota(jnp.int32, (rows, rows), 1)
    ).astype(jnp.bfloat16)
    before = jnp.dot(named.astype(jnp.bfloat16), upto, preferred_element_type=jnp.float32)
    return jnp.sum(jnp.where(named, before.astype(jnp.int32) - 1, 0), axis=0, keepdims=True)


def place_body(slot, amplitudes, out):
    size = out.shape[0]
    wanted = lax.broadcasted_iota(jnp.int32, (size, slot.shape[1]), 0) + pl.program_id(0) * size
    pick = (slot[...] == wanted).astype(jnp.float32).astype(jnp.bfloat16)
    out[...] = jnp.dot(pick, amplitudes[...], preferred_element_type=jnp.float32).astype(out.dtype)


def place(slot, amplitudes, count):
    rows, depth = amplitudes.shape
    size = 256
    return pl.pallas_call(
        place_body,
        grid=(count // size,),
        in_specs=[
            pl.BlockSpec(slot.shape, lambda i: (0, 0)),
            pl.BlockSpec((rows, depth), lambda i: (0, 0)),
        ],
        out_specs=pl.BlockSpec((size, depth), lambda i: (i, 0)),
        out_shape=jax.ShapeDtypeStruct((count, depth), jnp.bfloat16),
        compiler_params=pltpu.CompilerParams(vmem_limit_bytes=24 << 20),
        cost_estimate=pl.CostEstimate(
            flops=2 * count * rows * depth, bytes_accessed=2 * (rows + count) * depth, transcendentals=0
        ),
    )(slot, amplitudes)


def multiply_body(x, w, out):
    out[...] = jnp.dot(x[...], w[...], preferred_element_type=jnp.float32).astype(out.dtype)


def multiply(x, w):
    count, depth = x.shape
    columns = w.shape[1]
    size = 256
    return pl.pallas_call(
        multiply_body,
        grid=(count // size,),
        in_specs=[
            pl.BlockSpec((size, depth), lambda i: (i, 0)),
            pl.BlockSpec((depth, columns), lambda i: (0, 0)),
        ],
        out_specs=pl.BlockSpec((size, columns), lambda i: (i, 0)),
        out_shape=jax.ShapeDtypeStruct((count, columns), jnp.bfloat16),
        compiler_params=pltpu.CompilerParams(vmem_limit_bytes=32 << 20),
        cost_estimate=pl.CostEstimate(
            flops=2 * count * depth * columns,
            bytes_accessed=2 * (count * (depth + columns) + depth * columns), transcendentals=0,
        ),
    )(x, w)


def local(amplitudes, integrals, pair_class):
    n_class = lax.axis_size("vp")
    rows = amplitudes.shape[0]
    w = integrals[0]
    classes = pair_class.reshape(1, rows)
    position = row_positions(classes, n_class)

    def exchange(x):
        return lax.all_to_all(x, "vp", split_axis=0, concat_axis=0, tiled=True)

    slots, summed = [], []
    first = 0
    for size in CHUNKS:
        here = (position >= first) & (position < first + size)
        slots.append(jnp.where(here, classes * size + position - first, -1))
        partial = multiply(exchange(place(slots[-1], amplitudes, n_class * size)), w)
        summed.append(lax.psum_scatter(partial, "op", scatter_dimension=1, tiled=True))
        first += size
    out = 0
    for slot, x in zip(slots, summed):
        back = exchange(x)
        pick = (slot == lax.broadcasted_iota(jnp.int32, (back.shape[0], rows), 0)).astype(jnp.bfloat16)
        out = out + lax.dot_general(
            back, pick, (((0,), (0,)), ((), ())), preferred_element_type=jnp.float32
        )
    return out.astype(jnp.bfloat16)


def solution(mesh):
    return jax.shard_map(
        local,
        mesh=mesh,
        in_specs=(P("vp", "op"), P("vp", "op", None), P("vp", None)),
        out_specs=P("op", "vp"),
        check_vma=False,
    )
```

time: 298 us -> 252 us (0.85)
  matrix products: 72.9 us -> 3.98 us
  Pallas kernels: 0 us -> 40.4 us
  blocking collectives: 152 us -> 134 us
  local copies, waits for them, and re-layouts: 0.01 us -> 10.7 us
  starting transfers between devices: 18.7 us -> 10.4 us
    dot_general x16 -> x3, matrix products: 72.9 us -> 3.98 us  [the longest x2 2.87 us: local(): lax.dot_general(back, pick, (((0,), (0,)), ((), ())), preferred_element_t...]
    pallas_call x0 -> x4, Pallas kernels: none -> 40.4 us  [the longest x2 27.7 us: multiply(): pl.pallas_call(multiply_body, grid=(count // size,), in_specs=[pl.BlockSp...]
    all_to_all x5 -> x2, waiting for transfers between devices: 39.1 us -> 7.99 us  [exchange(): return lax.all_to_all(x, 'vp', split_axis=0, concat_axis=0, tiled=True)]
    reduce_scatter x5 -> x2, waiting for transfers between devices: 0.1 us -> 29.7 us  [local(): lax.psum_scatter(partial, 'op', scatter_dimension=1, tiled=True)]
    all_to_all x5 -> x2, blocking collectives: 152 us -> 134 us  [exchange(): return lax.all_to_all(x, 'vp', split_axis=0, concat_axis=0, tiled=True)]
    unnamed x4 -> x10, local copies, waits for them, and re-layouts: 0.01 us -> 10.7 us
    all_to_all x5 -> x2, starting transfers between devices: 18.5 us -> 10.3 us  [exchange(): return lax.all_to_all(x, 'vp', split_axis=0, concat_axis=0, tiled=True)]
  transfers between devices with their start and end apart: 10 -> 4, of which waited for: 5 -> 2; matrix products, arithmetic and copies ran while one was open for 20% -> 1% of each run, Pallas kernels for 0% -> 5%
where the time goes in v3:
time: 252 us
  blocking collectives  134 us (53%)
  Pallas kernels  40.4 us (16%)
  waiting for transfers between devices  37.7 us (15%)
  between operations  13.5 us (5%)
  local copies, waits for them, and re-layouts  10.7 us (4%)
  starting transfers between devices  10.4 us (4%)
  matrix products  3.98 us (2%)
    all_to_all x2, blocking collectives, exchange(): return lax.all_to_all(x, 'vp', split_axis=0, concat_axis=0, tiled=True)  134 us
    reduce_scatter x2, waiting for transfers between devices, local(): lax.psum_scatter(partial, 'op', scatter_dimension=1, tiled=True)  29.7 us
    pallas_call x2, Pallas kernels, multiply(): pl.pallas_call(multiply_body, grid=(count // size,), in_specs=[pl.BlockSp...  27.7 us
    pallas_call x2, Pallas kernels, place(): pl.pallas_call(place_body, grid=(count // size,), in_specs=[pl.BlockSpec(...  12.7 us
    unnamed x10, local copies, waits for them, and re-layouts  10.7 us
    all_to_all x2, starting transfers between devices, exchange(): return lax.all_to_all(x, 'vp', split_axis=0, concat_axis=0, tiled=True)  10.3 us
    all_to_all x2, waiting for transfers between devices, exchange(): return lax.all_to_all(x, 'vp', split_axis=0, concat_axis=0, tiled=True)  7.99 us
  transfers between devices with their start and end apart: 4, of which 2 were waited for; matrix products, arithmetic and copies ran while one was open for 1% of the time, Pallas kernels for 5%

profile of v3, /device:TPU:0, one launch (start us, length us, event | category | flops | bytes accessed | tf_op | source)
XLA Modules:
  0.0 251.9 jit_solution(3815136336055329441)
XLA Ops:
  6.5 1.1 fusion.10
  7.7 0.7 and_select_fusion
  8.4 0.0 copy-start.2
  8.4 2.2 copy-done.2
  10.6 8.9 %shard_map.37 = bf16[1792,2048]{1,0:T(8,128)(2,1)S(1)} custom-call(s32[1,1024]{1,0:T(1,128)S(1)} %get-tuple-element.8.slot, bf16[1024,2048]{1,0:T(8,128)(2,1)S(1)} %copy-done.2), custom_call_target="tpu_custom_call" | custom-call | flops 7516192768 | bytes 11534336 | tf_op jit(solution)/shard_map/pallas_call | solution.py:34
  19.4 92.5 %all_to_all.46 = bf16[16,112,2048]{2,1,0:T(8,128)(2,1)S(1)} all-to-all(bf16[16,112,2048]{2,1,0:T(8,128)(2,1)S(1)} %bitcast.23), channel_id=1, replica_groups=mesh['vp'=16,'op'=8] {'vp'}, dimensions={0} | all-to-all | bytes 14680064 | tf_op jit(solution)/shard_map/all_to_all | solution.py:83
  111.9 19.7 %shard_map.38 = bf16[1792,2048]{1,0:T(8,128)(2,1)S(1)} custom-call(bf16[1792,2048]{1,0:T(8,128)(2,1)S(1)} %bitcast.24, bf16[2048,2048]{1,0:T(8,128)(2,1)} %bitcast.27), custom_call_target="tpu_custom_call" | custom-call | flops 15032385536 | bytes 23068672 | tf_op jit(solution)/shard_map/pallas_call | solution.py:58
  131.7 2.9 %copy-done = bf16[1792,2048]{1,0:T(8,128)(2,1)} copy-done((bf16[1792,2048]{1,0:T(8,128)(2,1)}, bf16[1792,2048]{1,0:T(8,128)(2,1)S(1)}, u32[]{:S(2)}) %copy-start) | copy-done | bytes 7340056
  134.6 0.0 reduce-scatter.3.cloned.1.call-update
  134.6 0.0 reduce-scatter.5.cloned.1.call-start
  134.7 0.0 copy-start.3
  134.7 2.2 copy-done.3
  136.9 3.8 %shard_map.39 = bf16[768,2048]{1,0:T(8,128)(2,1)S(1)} custom-call(s32[1,1024]{1,0:T(1,128)S(1)} %get-tuple-element.7.slot, bf16[1024,2048]{1,0:T(8,128)(2,1)S(1)} %copy-done.3), custom_call_target="tpu_custom_call" | custom-call | flops 3221225472 | bytes 7340032 | tf_op jit(solution)/shard_map/pallas_call | solution.py:34
  140.7 42.0 %all_to_all.47 = bf16[16,48,2048]{2,1,0:T(8,128)(2,1)S(1)} all-to-all(bf16[16,48,2048]{2,1,0:T(8,128)(2,1)S(1)} %bitcast.25), channel_id=1, replica_groups=mesh['vp'=16,'op'=8] {'vp'}, dimensions={0} | all-to-all | bytes 6291456 | tf_op jit(solution)/shard_map/all_to_all | solution.py:83
  182.7 3.4 %copy-done.1 = bf16[1,2048,2048]{2,1,0:T(8,128)(2,1)S(1)} copy-done((bf16[1,2048,2048]{2,1,0:T(8,128)(2,1)S(1)}, bf16[1,2048,2048]{2,1,0:T(8,128)(2,1)}, u32[]{:S(2)}) %copy-start.1) | copy-done | bytes 8388632
  186.1 8.0 %shard_map.40 = bf16[768,2048]{1,0:T(8,128)(2,1)} custom-call(bf16[768,2048]{1,0:T(8,128)(2,1)S(1)} %bitcast.26, bf16[2048,2048]{1,0:T(8,128)(2,1)S(1)} %bitcast.28), custom_call_target="tpu_custom_call" | custom-call | flops 6442450944 | bytes 14680064 | tf_op jit(solution)/shard_map/pallas_call | solution.py:58
  194.0 0.0 reduce-scatter.5.cloned.1.call-update
  194.1 0.0 reduce-scatter.3.cloned.1.call-done
  194.1 3.6 %all-to-all-start.1 = ((bf16[16,112,256]{2,1,0:T(8,128)(2,1)}), bf16[16,112,256]{2,1,0:T(8,128)(2,1)S(1)}, u32[]{:S(2)}, u32[]{:S(2)}) async-start(bf16[16,112,256]{2,1,0:T(8,128)(2,1)} %bitcast.29), calls=%async_computation.2 | async-start | bytes 1835008 | tf_op jit(solution)/shard_map/all_to_all | solution.py:83
  197.7 29.7 %reduce-scatter.5.cloned.1.call-done = bf16[768,256]{1,0:T(8,128)(2,1)} async-done(((bf16[768,2048]{1,0:T(8,128)(2,1)}), bf16[768,256]{1,0:T(8,128)(2,1)}) %reduce-scatter.5.cloned.1.call-update) | async-done | bytes 393232 | tf_op jit(solution)/shard_map/reduce_scatter | solution.py:91
  227.4 6.7 %all-to-all-start.3 = ((bf16[16,48,256]{2,1,0:T(8,128)(2,1)}), bf16[16,48,256]{2,1,0:T(8,128)(2,1)S(1)}, u32[]{:S(2)}, u32[]{:S(2)}) async-start(bf16[16,48,256]{2,1,0:T(8,128)(2,1)} %bitcast.31), calls=%async_computation.5 | async-start | bytes 786432 | tf_op jit(solution)/shard_map/all_to_all | solution.py:83
  234.2 1.4 fusion
  235.5 8.0 %all-to-all-done.3 = bf16[16,48,256]{2,1,0:T(8,128)(2,1)S(1)} async-done(((bf16[16,48,256]{2,1,0:T(8,128)(2,1)}), bf16[16,48,256]{2,1,0:T(8,128)(2,1)S(1)}, u32[]{:S(2)}, u32[]{:S(2)}) %all-to-all-start.3) | async-done | bytes 393248 | tf_op jit(solution)/shard_map/all_to_all | solution.py:83
  243.5 1.5 fusion.6
  (7 shorter events, 0.0 us)
Async XLA Ops:
  6.5 187.5 %reduce-scatter.3.cloned.1.call-start = ((), (), s32[]{:S(2)}) async-start(), calls=%async_computation.6 | async-start | bytes 8257536 | tf_op jit(solution)/shard_map/reduce_scatter | solution.py:91
  8.4 2.2 copy-start.2
  131.7 2.9 %copy-start = (bf16[1792,2048]{1,0:T(8,128)(2,1)}, bf16[1792,2048]{1,0:T(8,128)(2,1)S(1)}, u32[]{:S(2)}) copy-start(bf16[1792,2048]{1,0:T(8,128)(2,1)S(1)} %shard_map.38) | copy-start | bytes 22020100
  134.6 92.8 %reduce-scatter.5.cloned.1.call-start = ((), (), s32[]{:S(2)}) async-start(), calls=%async_computation.7 | async-start | bytes 3538944 | tf_op jit(solution)/shard_map/reduce_scatter | solution.py:91
  134.7 2.2 copy-start.3
  182.7 3.4 %copy-start.1 = (bf16[1,2048,2048]{2,1,0:T(8,128)(2,1)S(1)}, bf16[1,2048,2048]{2,1,0:T(8,128)(2,1)}, u32[]{:S(2)}) copy-start(bf16[1,2048,2048]{2,1,0:T(8,128)(2,1)} %param.4) | copy-start | bytes 25165828
  194.0 40.1 %copy-start.4 = (s32[1024,1]{0,1:T(1,128)S(1)}, s32[1024,1]{0,1:T(1,128)}, u32[]{:S(2)}) copy-start(s32[1024,1]{0,1:T(1,128)} %param.5) | copy-start | bytes 12292
  194.1 33.3 %all-to-all-start.1 = ((bf16[16,112,256]{2,1,0:T(8,128)(2,1)}), bf16[16,112,256]{2,1,0:T(8,128)(2,1)S(1)}, u32[]{:S(2)}, u32[]{:S(2)}) async-start(bf16[16,112,256]{2,1,0:T(8,128)(2,1)} %bitcast.29), calls=%async_computation.2 | async-start | bytes 1835008 | tf_op jit(solution)/shard_map/all_to_all | solution.py:83
  227.4 16.1 %all-to-all-start.3 = ((bf16[16,48,256]{2,1,0:T(8,128)(2,1)}), bf16[16,48,256]{2,1,0:T(8,128)(2,1)S(1)}, u32[]{:S(2)}, u32[]{:S(2)}) async-start(bf16[16,48,256]{2,1,0:T(8,128)(2,1)} %bitcast.31), calls=%async_computation.5 | async-start | bytes 786432 | tf_op jit(solution)/shard_map/all_to_all | solution.py:83
Sparse Core Ops, SparseCore 0:
  134.8 44.8 reduce-scatter.2
  194.2 33.1 reduce-scatter.4

commit v4 on v3

--- a/solution.py
+++ b/solution.py
@@ -7,7 +7,9 @@
 from jax.experimental.pallas import tpu as pltpu
 from jax.sharding import PartitionSpec as P
 
-CHUNKS = (112, 48)
+CHUNKS = (128, 32)
+CORES = 2
+BLOCK = 256
 
 
 def row_positions(classes, n_class):
@@ -64,12 +66,55 @@
         ],
         out_specs=pl.BlockSpec((size, columns), lambda i: (i, 0)),
         out_shape=jax.ShapeDtypeStruct((count, columns), jnp.bfloat16),
-        compiler_params=pltpu.CompilerParams(vmem_limit_bytes=32 << 20),
+        compiler_params=pltpu.CompilerParams(vmem_limit_bytes=56 << 20),
         cost_estimate=pl.CostEstimate(
             flops=2 * count * depth * columns,
             bytes_accessed=2 * (count * (depth + columns) + depth * columns), transcendentals=0,
         ),
     )(x, w)
+
+
+def add_body(n, *refs):
+    total = refs[0][...].astype(jnp.float32)
+    for ref in refs[1:n]:
+        total = total + ref[...].astype(jnp.float32)
+    total = total.astype(jnp.bfloat16)
+    width = refs[n].shape[1]
+    for k, out in enumerate(refs[n:]):
+        out[...] = total[:, k * width : (k + 1) * width]
+
+
+def add(terms, width):
+    count, columns = terms[0].shape
+    return pl.pallas_call(
+        functools.partial(add_body, len(terms)),
+        grid=(count // BLOCK,),
+        in_specs=[pl.BlockSpec((BLOCK, columns), lambda i: (i, 0))] * len(terms),
+        out_specs=[pl.BlockSpec((BLOCK, width), lambda i: (i, 0))] * (columns // width),
+        out_shape=[jax.ShapeDtypeStruct((count, width), jnp.bfloat16)] * (columns // width),
+        compiler_params=pltpu.CompilerParams(vmem_limit_bytes=16 << 20),
+    )(*terms)
+
+
+def sum_over_op(partial):
+    n_op = lax.axis_size("op")
+    n_x = n_op // CORES
+    me = lax.axis_index("op")
+    width = partial.shape[1] // n_op
+
+    def columns(core):
+        blocks = [((me // CORES + d) % n_x * CORES + core) * width for d in range(n_x)]
+        return jnp.concatenate([lax.dynamic_slice_in_dim(partial, b, width, 1) for b in blocks], axis=1)
+
+    mine, other = columns(me % CORES), columns(1 - me % CORES)
+
+    def permute(x, dx, swap):
+        to = [(o // CORES + dx) % n_x * CORES + (o + swap) % CORES for o in range(n_op)]
+        return lax.ppermute(x, "op", list(enumerate(to)))
+
+    blocks = add([mine, permute(other, 0, 1)], mine.shape[1] // n_x)
+    terms = [blocks[0]] + [permute(blocks[d], d, 0) for d in range(1, n_x)]
+    return add(terms, blocks[0].shape[1])[0]
 
 
 def local(amplitudes, integrals, pair_class):
@@ -88,7 +133,10 @@
         here = (position >= first) & (position < first + size)
         slots.append(jnp.where(here, classes * size + position - first, -1))
         partial = multiply(exchange(place(slots[-1], amplitudes, n_class * size)), w)
-        summed.append(lax.psum_scatter(partial, "op", scatter_dimension=1, tiled=True))
+        if first + size < sum(CHUNKS):
+            summed.append(lax.psum_scatter(partial, "op", scatter_dimension=1, tiled=True))
+        else:
+            summed.append(sum_over_op(partial))
         first += size
     out = 0
     for slot, x in zip(slots, summed):

time: 252 us -> 247 us (0.980)
  blocking collectives: 134 us -> 104 us
  waiting for transfers between devices: 37.7 us -> 47.5 us
  starting transfers between devices: 10.4 us -> 20 us
  Pallas kernels: 40.4 us -> 47.7 us
  local copies, waits for them, and re-layouts: 10.7 us -> 8.17 us
    all_to_all x2 -> x1, blocking collectives: 134 us -> 104 us  [exchange(): return lax.all_to_all(x, 'vp', split_axis=0, concat_axis=0, tiled=True)]
    reduce_scatter x2 -> x1, waiting for transfers between devices: 29.7 us -> 0.02 us  [local(): lax.psum_scatter(partial, 'op', scatter_dimension=1, tiled=True)]
    all_to_all x2 -> x3, waiting for transfers between devices: 7.99 us -> 36.6 us  [exchange(): return lax.all_to_all(x, 'vp', split_axis=0, concat_axis=0, tiled=True)]
    ppermute x0 -> x4, waiting for transfers between devices: none -> 10.8 us  [permute(): return lax.ppermute(x, 'op', list(enumerate(to)))]
    pallas_call x2, Pallas kernels: 27.7 us -> 33 us  [multiply(): pl.pallas_call(multiply_body, grid=(count // size,), in_specs=[pl.BlockSp...]
    ppermute x0 -> x4, starting transfers between devices: none -> 5 us  [permute(): return lax.ppermute(x, 'op', list(enumerate(to)))]
    unnamed x10 -> x8, local copies, waits for them, and re-layouts: 10.7 us -> 5.7 us
    all_to_all x2 -> x3, starting transfers between devices: 10.3 us -> 15 us  [exchange(): return lax.all_to_all(x, 'vp', split_axis=0, concat_axis=0, tiled=True)]
  transfers between devices with their start and end apart: 4 -> 8, of which waited for: 2 -> 4; matrix products, arithmetic and copies ran while one was open for 1% -> 2% of each run, Pallas kernels for 5% -> 6%
where the time goes in v4:
time: 247 us
  blocking collectives  104 us (42%)
  Pallas kernels  47.7 us (19%)
  waiting for transfers between devices  47.5 us (19%)
  starting transfers between devices  20 us (8%)
  between operations  13.6 us (6%)
  local copies, waits for them, and re-layouts  8.17 us (3%)
  matrix products  3.98 us (2%)
    all_to_all x1, blocking collectives, exchange(): return lax.all_to_all(x, 'vp', split_axis=0, concat_axis=0, tiled=True)  104 us
    all_to_all x3, waiting for transfers between devices, exchange(): return lax.all_to_all(x, 'vp', split_axis=0, concat_axis=0, tiled=True)  36.6 us
    pallas_call x2, Pallas kernels, multiply(): pl.pallas_call(multiply_body, grid=(count // size,), in_specs=[pl.BlockSp...  33 us
    all_to_all x3, starting transfers between devices, exchange(): return lax.all_to_all(x, 'vp', split_axis=0, concat_axis=0, tiled=True)  15 us
    pallas_call x2, Pallas kernels, place(): pl.pallas_call(place_body, grid=(count // size,), in_specs=[pl.BlockSpec(...  13.6 us
    ppermute x4, waiting for transfers between devices, permute(): return lax.ppermute(x, 'op', list(enumerate(to)))  10.8 us
    unnamed x8, local copies, waits for them, and re-layouts  5.7 us
    ppermute x4, starting transfers between devices, permute(): return lax.ppermute(x, 'op', list(enumerate(to)))  5 us
  transfers between devices with their start and end apart: 8, of which 4 were waited for; matrix products, arithmetic and copies ran while one was open for 2% of the time, Pallas kernels for 6%

profile of v4, /device:TPU:0, one launch (start us, length us, event | category | flops | bytes accessed | tf_op | source)
XLA Modules:
  0.0 246.9 jit_solution(16610186291648921518)
XLA Ops:
  6.5 1.1 fusion.9
  8.4 2.2 copy-done
  10.6 10.1 %shard_map.37 = bf16[2048,2048]{1,0:T(8,128)(2,1)S(1)} custom-call(s32[1,1024]{1,0:T(1,128)S(1)} %get-tuple-element.24.slot, bf16[1024,2048]{1,0:T(8,128)(2,1)S(1)} %copy-done), custom_call_target="tpu_custom_call" | custom-call | flops 8589934592 | bytes 12582912 | tf_op jit(solution)/shard_map/pallas_call | solution.py:36
  20.7 103.8 %all_to_all.46 = bf16[16,128,2048]{2,1,0:T(8,128)(2,1)} all-to-all(bf16[16,128,2048]{2,1,0:T(8,128)(2,1)S(1)} %bitcast.23), channel_id=1, replica_groups=mesh['vp'=16,'op'=8] {'vp'}, dimensions={0} | all-to-all | bytes 16777216 | tf_op jit(solution)/shard_map/all_to_all | solution.py:128
  124.5 23.5 %shard_map.38 = bf16[2048,2048]{1,0:T(8,128)(2,1)} custom-call(bf16[2048,2048]{1,0:T(8,128)(2,1)} %bitcast.24, bf16[2048,2048]{1,0:T(8,128)(2,1)} %bitcast.32), custom_call_target="tpu_custom_call" | custom-call | flops 17179869184 | bytes 25165824 | tf_op jit(solution)/shard_map/pallas_call | solution.py:60
  148.0 2.2 copy-done.1
  150.2 3.5 %shard_map.39 = bf16[512,2048]{1,0:T(8,128)(2,1)} custom-call(s32[1,1024]{1,0:T(1,128)S(1)} %get-tuple-element.23.slot, bf16[1024,2048]{1,0:T(8,128)(2,1)S(1)} %copy-done.1), custom_call_target="tpu_custom_call" | custom-call | flops 2147483648 | bytes 6291456 | tf_op jit(solution)/shard_map/pallas_call | solution.py:36
  153.7 3.7 %all-to-all-start.2 = ((bf16[16,32,2048]{2,1,0:T(8,128)(2,1)}), bf16[16,32,2048]{2,1,0:T(8,128)(2,1)S(1)}, u32[]{:S(2)}, u32[]{:S(2)}) async-start(bf16[16,32,2048]{2,1,0:T(8,128)(2,1)} %bitcast.9), calls=%async_computation.3 | async-start | bytes 4194304 | tf_op jit(solution)/shard_map/all_to_all | solution.py:128
  157.6 29.5 %all-to-all-done.2 = bf16[16,32,2048]{2,1,0:T(8,128)(2,1)S(1)} async-done(((bf16[16,32,2048]{2,1,0:T(8,128)(2,1)}), bf16[16,32,2048]{2,1,0:T(8,128)(2,1)S(1)}, u32[]{:S(2)}, u32[]{:S(2)}) %all-to-all-start.2) | async-done | bytes 2097184 | tf_op jit(solution)/shard_map/all_to_all | solution.py:128
  187.0 1.3 copy-done.2
  188.3 9.5 %shard_map.40 = bf16[512,2048]{1,0:T(8,128)(2,1)} custom-call(bf16[512,2048]{1,0:T(8,128)(2,1)} %bitcast.25, bf16[2048,2048]{1,0:T(8,128)(2,1)} %bitcast.33), custom_call_target="tpu_custom_call" | custom-call | flops 4294967296 | bytes 12582912 | tf_op jit(solution)/shard_map/pallas_call | solution.py:60
  197.9 2.5 %constant_dynamic-slice_fusion.2 = (bf16[512,256]{1,0:T(8,128)(2,1)S(1)}, bf16[512,256]{1,0:T(8,128)(2,1)S(1)}, bf16[512,256]{1,0:T(8,128)(2,1)S(1)}, bf16[512,2...) fusion(bf16[512,2048]{1,0:T(8,128)(2,1)} %shard_map.40, ...), kind=kLoop, calls=%fused_computation.27 | loop fusion | bytes 4194336 | tf_op jit(solution)/shard_map/dynamic_slice | solution.py:107
  200.6 4.4 %all-to-all-start.1 = ((bf16[16,128,256]{2,1,0:T(8,128)(2,1)}), bf16[16,128,256]{2,1,0:T(8,128)(2,1)S(1)}, u32[]{:S(2)}, u32[]{:S(2)}) async-start(bf16[16,128,256]{2,1,0:T(8,128)(2,1)} %bitcast.26), calls=%async_computation.2 | async-start | bytes 2097152 | tf_op jit(solution)/shard_map/all_to_all | solution.py:128
  205.1 1.2 pad_maximum_fusion.refs_0_
  206.6 0.8 collective-permute-start.1
  207.4 2.6 %collective-permute-start.2 = (bf16[512,256]{1,0:T(8,128)(2,1)S(1)}, bf16[512,256]{1,0:T(8,128)(2,1)S(1)}, u32[]{:S(2)}, u32[]{:S(2)}) collective-permute-start(bf16[512,256]{1,0:T(8,128)(2,1)S(1)} %get-tuple-element.11), channel_id=1, source_target_pairs={{0,4},{1,5},{2,6},{3,7},{4,0},{5,1},{6,2},{7,3},{8,12},{9,13},{10,... | collective-permute-start | bytes 786440 | tf_op jit(solution)/shard_map/ppermute | solution.py:113
  210.1 1.4 collective-permute-start.3
  211.5 4.3 %collective-permute-done.1.refs_1_ = bf16[512,256]{1,0:T(8,128)(2,1)S(1)} collective-permute-done((bf16[512,256]{1,0:T(8,128)(2,1)S(1)}, bf16[512,256]{1,0:T(8,128)(2,1)S(1)}, u32[]{:S(2)}, u32[]{:S(2)}) %collective-permute-start.1) | collective-permute-done | bytes 262176 | tf_op jit(solution)/shard_map/ppermute | solution.py:113
  215.8 6.5 %collective-permute-done.2.refs_2_ = bf16[512,256]{1,0:T(8,128)(2,1)S(1)} collective-permute-done((bf16[512,256]{1,0:T(8,128)(2,1)S(1)}, bf16[512,256]{1,0:T(8,128)(2,1)S(1)}, u32[]{:S(2)}, u32[]{:S(2)}) %collective-permute-start.2) | collective-permute-done | bytes 262176 | tf_op jit(solution)/shard_map/ppermute | solution.py:113
  222.4 0.8 shard_map.42
  223.2 6.9 %all-to-all-start.3 = ((bf16[16,32,256]{2,1,0:T(8,128)(2,1)}), bf16[16,32,256]{2,1,0:T(8,128)(2,1)S(1)}, u32[]{:S(2)}, u32[]{:S(2)}) async-start(bf16[16,32,256]{2,1,0:T(8,128)(2,1)} %bitcast.11), calls=%async_computation.4 | async-start | bytes 524288 | tf_op jit(solution)/shard_map/all_to_all | solution.py:128
  230.1 1.5 fusion
  231.6 7.1 %all-to-all-done.3 = bf16[16,32,256]{2,1,0:T(8,128)(2,1)S(1)} async-done(((bf16[16,32,256]{2,1,0:T(8,128)(2,1)}), bf16[16,32,256]{2,1,0:T(8,128)(2,1)S(1)}, u32[]{:S(2)}, u32[]{:S(2)}) %all-to-all-start.3) | async-done | bytes 262176 | tf_op jit(solution)/shard_map/all_to_all | solution.py:128
  238.7 1.3 fusion.5
  (16 shorter events, 1.3 us)
Async XLA Ops:
  6.5 194.1 %reduce-scatter.2.cloned.1.call-start = ((), (), s32[]{:S(2)}) async-start(), calls=%async_computation.5 | async-start | bytes 9437184 | tf_op jit(solution)/shard_map/reduce_scatter | solution.py:137
  8.4 2.2 copy-start
  148.0 2.2 copy-start.1
  153.7 33.3 %all-to-all-start.2 = ((bf16[16,32,2048]{2,1,0:T(8,128)(2,1)}), bf16[16,32,2048]{2,1,0:T(8,128)(2,1)S(1)}, u32[]{:S(2)}, u32[]{:S(2)}) async-start(bf16[16,32,2048]{2,1,0:T(8,128)(2,1)} %bitcast.9), calls=%async_computation.3 | async-start | bytes 4194304 | tf_op jit(solution)/shard_map/all_to_all | solution.py:128
  187.0 1.3 copy-start.2
  200.5 5.8 %collective-permute-start = (bf16[512,1024]{1,0:T(8,128)(2,1)S(1)}, bf16[512,1024]{1,0:T(8,128)(2,1)S(1)}, u32[]{:S(2)}, u32[]{:S(2)}) collective-permute-start(bf16[512,1024]{1,0:T(8,128)(2,1)S(1)} %pad_maximum_fusion.1), channel_id=1, source_target_pairs={{0,1},{1,0},{2,3},{3,2},{4,5},{5,4},{6,7},{7,6},{8,9},{9,8},{10,11... | collective-permute-start | bytes 3145736 | tf_op jit(solution)/shard_map/ppermute | solution.py:113
  200.6 22.5 %all-to-all-start.1 = ((bf16[16,128,256]{2,1,0:T(8,128)(2,1)}), bf16[16,128,256]{2,1,0:T(8,128)(2,1)S(1)}, u32[]{:S(2)}, u32[]{:S(2)}) async-start(bf16[16,128,256]{2,1,0:T(8,128)(2,1)} %bitcast.26), calls=%async_computation.2 | async-start | bytes 2097152 | tf_op jit(solution)/shard_map/all_to_all | solution.py:128
  205.0 6.5 %copy-start.3 = (s32[1024,1]{0,1:T(1,128)S(1)}, s32[1024,1]{0,1:T(1,128)}, u32[]{:S(2)}) copy-start(s32[1024,1]{0,1:T(1,128)} %param.5) | copy-start | bytes 12292
  206.6 9.2 %collective-permute-start.1 = (bf16[512,256]{1,0:T(8,128)(2,1)S(1)}, bf16[512,256]{1,0:T(8,128)(2,1)S(1)}, u32[]{:S(2)}, u32[]{:S(2)}) collective-permute-start(bf16[512,256]{1,0:T(8,128)(2,1)S(1)} %get-tuple-element.10), channel_id=1, source_target_pairs={{0,2},{1,3},{2,4},{3,5},{4,6},{5,7},{6,0},{7,1},{8,10},{9,11},{10,... | collective-permute-start | bytes 786440 | tf_op jit(solution)/shard_map/ppermute | solution.py:113
  207.4 14.9 %collective-permute-start.2 = (bf16[512,256]{1,0:T(8,128)(2,1)S(1)}, bf16[512,256]{1,0:T(8,128)(2,1)S(1)}, u32[]{:S(2)}, u32[]{:S(2)}) collective-permute-start(bf16[512,256]{1,0:T(8,128)(2,1)S(1)} %get-tuple-element.11), channel_id=1, source_target_pairs={{0,4},{1,5},{2,6},{3,7},{4,0},{5,1},{6,2},{7,3},{8,12},{9,13},{10,... | collective-permute-start | bytes 786440 | tf_op jit(solution)/shard_map/ppermute | solution.py:113
  210.1 12.3 %collective-permute-start.3 = (bf16[512,256]{1,0:T(8,128)(2,1)S(1)}, bf16[512,256]{1,0:T(8,128)(2,1)S(1)}, u32[]{:S(2)}, u32[]{:S(2)}) collective-permute-start(bf16[512,256]{1,0:T(8,128)(2,1)S(1)} %get-tuple-element.12), channel_id=1, source_target_pairs={{0,6},{1,7},{2,0},{3,1},{4,2},{5,3},{6,4},{7,5},{8,14},{9,15},{10,... | collective-permute-start | bytes 786440 | tf_op jit(solution)/shard_map/ppermute | solution.py:113
  223.2 15.6 %all-to-all-start.3 = ((bf16[16,32,256]{2,1,0:T(8,128)(2,1)}), bf16[16,32,256]{2,1,0:T(8,128)(2,1)S(1)}, u32[]{:S(2)}, u32[]{:S(2)}) async-start(bf16[16,32,256]{2,1,0:T(8,128)(2,1)} %bitcast.11), calls=%async_computation.4 | async-start | bytes 524288 | tf_op jit(solution)/shard_map/all_to_all | solution.py:128
Sparse Core Ops, SparseCore 0:
  148.1 49.8 reduce-scatter.1

commit v5 on v4

--- a/solution.py
+++ b/solution.py
@@ -56,7 +56,7 @@
 def multiply(x, w):
     count, depth = x.shape
     columns = w.shape[1]
-    size = 256
+    size = 512
     return pl.pallas_call(
         multiply_body,
         grid=(count // size,),

time: 247 us -> 248 us (level)
  no operation moved by 1% of the time
where the time goes in v5:
time: 248 us; the launch traced here: 247 us
  blocking collectives  104 us (42%)
  Pallas kernels  48.1 us (19%)
  waiting for transfers between devices  47.5 us (19%)
  starting transfers between devices  20 us (8%)
  between operations  13.6 us (5%)
  local copies, waits for them, and re-layouts  8.17 us (3%)
  matrix products  3.98 us (2%)
    all_to_all x1, blocking collectives, exchange(): return lax.all_to_all(x, 'vp', split_axis=0, concat_axis=0, tiled=True)  104 us
    all_to_all x3, waiting for transfers between devices, exchange(): return lax.all_to_all(x, 'vp', split_axis=0, concat_axis=0, tiled=True)  36.6 us
    pallas_call x2, Pallas kernels, multiply(): pl.pallas_call(multiply_body, grid=(count // size,), in_specs=[pl.BlockSp...  33.4 us
    all_to_all x3, starting transfers between devices, exchange(): return lax.all_to_all(x, 'vp', split_axis=0, concat_axis=0, tiled=True)  14.5 us
    pallas_call x2, Pallas kernels, place(): pl.pallas_call(place_body, grid=(count // size,), in_specs=[pl.BlockSpec(...  13.6 us
    ppermute x4, waiting for transfers between devices, permute(): return lax.ppermute(x, 'op', list(enumerate(to)))  10.8 us
    unnamed x8, local copies, waits for them, and re-layouts  5.7 us
    ppermute x4, starting transfers between devices, permute(): return lax.ppermute(x, 'op', list(enumerate(to)))  5.55 us
  transfers between devices with their start and end apart: 8, of which 4 were waited for; matrix products, arithmetic and copies ran while one was open for 2% of the time, Pallas kernels for 6%

profile of v5, /device:TPU:0, one launch (start us, length us, event | category | flops | bytes accessed | tf_op | source)
XLA Modules:
  0.0 247.4 jit_solution(9434914948769582694)
XLA Ops:
  6.5 1.1 fusion.9
  8.4 2.2 copy-done
  10.6 10.1 %shard_map.37 = bf16[2048,2048]{1,0:T(8,128)(2,1)S(1)} custom-call(s32[1,1024]{1,0:T(1,128)S(1)} %get-tuple-element.24.slot, bf16[1024,2048]{1,0:T(8,128)(2,1)S(1)} %copy-done), custom_call_target="tpu_custom_call" | custom-call | flops 8589934592 | bytes 12582912 | tf_op jit(solution)/shard_map/pallas_call | solution.py:36
  20.7 103.8 %all_to_all.46 = bf16[16,128,2048]{2,1,0:T(8,128)(2,1)} all-to-all(bf16[16,128,2048]{2,1,0:T(8,128)(2,1)S(1)} %bitcast.23), channel_id=1, replica_groups=mesh['vp'=16,'op'=8] {'vp'}, dimensions={0} | all-to-all | bytes 16777216 | tf_op jit(solution)/shard_map/all_to_all | solution.py:128
  124.5 23.4 %shard_map.38 = bf16[2048,2048]{1,0:T(8,128)(2,1)} custom-call(bf16[2048,2048]{1,0:T(8,128)(2,1)} %bitcast.24, bf16[2048,2048]{1,0:T(8,128)(2,1)} %bitcast.32), custom_call_target="tpu_custom_call" | custom-call | flops 17179869184 | bytes 25165824 | tf_op jit(solution)/shard_map/pallas_call | solution.py:60
  147.9 2.2 copy-done.1
  150.1 3.5 %shard_map.39 = bf16[512,2048]{1,0:T(8,128)(2,1)} custom-call(s32[1,1024]{1,0:T(1,128)S(1)} %get-tuple-element.23.slot, bf16[1024,2048]{1,0:T(8,128)(2,1)S(1)} %copy-done.1), custom_call_target="tpu_custom_call" | custom-call | flops 2147483648 | bytes 6291456 | tf_op jit(solution)/shard_map/pallas_call | solution.py:36
  153.6 3.7 %all-to-all-start.2 = ((bf16[16,32,2048]{2,1,0:T(8,128)(2,1)}), bf16[16,32,2048]{2,1,0:T(8,128)(2,1)S(1)}, u32[]{:S(2)}, u32[]{:S(2)}) async-start(bf16[16,32,2048]{2,1,0:T(8,128)(2,1)} %bitcast.9), calls=%async_computation.3 | async-start | bytes 4194304 | tf_op jit(solution)/shard_map/all_to_all | solution.py:128
  157.5 29.5 %all-to-all-done.2 = bf16[16,32,2048]{2,1,0:T(8,128)(2,1)S(1)} async-done(((bf16[16,32,2048]{2,1,0:T(8,128)(2,1)}), bf16[16,32,2048]{2,1,0:T(8,128)(2,1)S(1)}, u32[]{:S(2)}, u32[]{:S(2)}) %all-to-all-start.2) | async-done | bytes 2097184 | tf_op jit(solution)/shard_map/all_to_all | solution.py:128
  186.9 1.3 copy-done.2
  188.2 10.1 %shard_map.40 = bf16[512,2048]{1,0:T(8,128)(2,1)} custom-call(bf16[512,2048]{1,0:T(8,128)(2,1)} %bitcast.25, bf16[2048,2048]{1,0:T(8,128)(2,1)} %bitcast.33), custom_call_target="tpu_custom_call" | custom-call | flops 4294967296 | bytes 12582912 | tf_op jit(solution)/shard_map/pallas_call | solution.py:60
  198.3 2.5 %constant_dynamic-slice_fusion.2 = (bf16[512,256]{1,0:T(8,128)(2,1)S(1)}, bf16[512,256]{1,0:T(8,128)(2,1)S(1)}, bf16[512,256]{1,0:T(8,128)(2,1)S(1)}, bf16[512,2...) fusion(bf16[512,2048]{1,0:T(8,128)(2,1)} %shard_map.40, ...), kind=kLoop, calls=%fused_computation.27 | loop fusion | bytes 4194336 | tf_op jit(solution)/shard_map/dynamic_slice | solution.py:107
  201.0 3.9 %all-to-all-start.1 = ((bf16[16,128,256]{2,1,0:T(8,128)(2,1)}), bf16[16,128,256]{2,1,0:T(8,128)(2,1)S(1)}, u32[]{:S(2)}, u32[]{:S(2)}) async-start(bf16[16,128,256]{2,1,0:T(8,128)(2,1)} %bitcast.26), calls=%async_computation.2 | async-start | bytes 2097152 | tf_op jit(solution)/shard_map/all_to_all | solution.py:128
  205.0 1.2 pad_maximum_fusion.refs_0_
  206.5 1.3 collective-permute-start.1
  207.9 2.7 %collective-permute-start.2 = (bf16[512,256]{1,0:T(8,128)(2,1)S(1)}, bf16[512,256]{1,0:T(8,128)(2,1)S(1)}, u32[]{:S(2)}, u32[]{:S(2)}) collective-permute-start(bf16[512,256]{1,0:T(8,128)(2,1)S(1)} %get-tuple-element.11), channel_id=1, source_target_pairs={{0,4},{1,5},{2,6},{3,7},{4,0},{5,1},{6,2},{7,3},{8,12},{9,13},{10,... | collective-permute-start | bytes 786440 | tf_op jit(solution)/shard_map/ppermute | solution.py:113
  210.6 1.4 collective-permute-start.3
  212.0 4.2 %collective-permute-done.1.refs_1_ = bf16[512,256]{1,0:T(8,128)(2,1)S(1)} collective-permute-done((bf16[512,256]{1,0:T(8,128)(2,1)S(1)}, bf16[512,256]{1,0:T(8,128)(2,1)S(1)}, u32[]{:S(2)}, u32[]{:S(2)}) %collective-permute-start.1) | collective-permute-done | bytes 262176 | tf_op jit(solution)/shard_map/ppermute | solution.py:113
  216.2 6.6 %collective-permute-done.2.refs_2_ = bf16[512,256]{1,0:T(8,128)(2,1)S(1)} collective-permute-done((bf16[512,256]{1,0:T(8,128)(2,1)S(1)}, bf16[512,256]{1,0:T(8,128)(2,1)S(1)}, u32[]{:S(2)}, u32[]{:S(2)}) %collective-permute-start.2) | collective-permute-done | bytes 262176 | tf_op jit(solution)/shard_map/ppermute | solution.py:113
  222.8 0.8 shard_map.42
  223.6 6.9 %all-to-all-start.3 = ((bf16[16,32,256]{2,1,0:T(8,128)(2,1)}), bf16[16,32,256]{2,1,0:T(8,128)(2,1)S(1)}, u32[]{:S(2)}, u32[]{:S(2)}) async-start(bf16[16,32,256]{2,1,0:T(8,128)(2,1)} %bitcast.11), calls=%async_computation.4 | async-start | bytes 524288 | tf_op jit(solution)/shard_map/all_to_all | solution.py:128
  230.5 1.5 fusion
  232.1 7.1 %all-to-all-done.3 = bf16[16,32,256]{2,1,0:T(8,128)(2,1)S(1)} async-done(((bf16[16,32,256]{2,1,0:T(8,128)(2,1)}), bf16[16,32,256]{2,1,0:T(8,128)(2,1)S(1)}, u32[]{:S(2)}, u32[]{:S(2)}) %all-to-all-start.3) | async-done | bytes 262176 | tf_op jit(solution)/shard_map/all_to_all | solution.py:128
  239.2 1.3 fusion.5
  (16 shorter events, 1.3 us)
Async XLA Ops:
  6.5 194.5 %reduce-scatter.2.cloned.1.call-start = ((), (), s32[]{:S(2)}) async-start(), calls=%async_computation.5 | async-start | bytes 9437184 | tf_op jit(solution)/shard_map/reduce_scatter | solution.py:137
  8.4 2.2 copy-start
  147.9 2.2 copy-start.1
  153.6 33.3 %all-to-all-start.2 = ((bf16[16,32,2048]{2,1,0:T(8,128)(2,1)}), bf16[16,32,2048]{2,1,0:T(8,128)(2,1)S(1)}, u32[]{:S(2)}, u32[]{:S(2)}) async-start(bf16[16,32,2048]{2,1,0:T(8,128)(2,1)} %bitcast.9), calls=%async_computation.3 | async-start | bytes 4194304 | tf_op jit(solution)/shard_map/all_to_all | solution.py:128
  186.9 1.3 copy-start.2
  200.9 5.3 %collective-permute-start = (bf16[512,1024]{1,0:T(8,128)(2,1)S(1)}, bf16[512,1024]{1,0:T(8,128)(2,1)S(1)}, u32[]{:S(2)}, u32[]{:S(2)}) collective-permute-start(bf16[512,1024]{1,0:T(8,128)(2,1)S(1)} %pad_maximum_fusion.1), channel_id=1, source_target_pairs={{0,1},{1,0},{2,3},{3,2},{4,5},{5,4},{6,7},{7,6},{8,9},{9,8},{10,11... | collective-permute-start | bytes 3145736 | tf_op jit(solution)/shard_map/ppermute | solution.py:113
  201.0 22.6 %all-to-all-start.1 = ((bf16[16,128,256]{2,1,0:T(8,128)(2,1)}), bf16[16,128,256]{2,1,0:T(8,128)(2,1)S(1)}, u32[]{:S(2)}, u32[]{:S(2)}) async-start(bf16[16,128,256]{2,1,0:T(8,128)(2,1)} %bitcast.26), calls=%async_computation.2 | async-start | bytes 2097152 | tf_op jit(solution)/shard_map/all_to_all | solution.py:128
  204.9 7.0 %copy-start.3 = (s32[1024,1]{0,1:T(1,128)S(1)}, s32[1024,1]{0,1:T(1,128)}, u32[]{:S(2)}) copy-start(s32[1024,1]{0,1:T(1,128)} %param.5) | copy-start | bytes 12292
  206.5 9.7 %collective-permute-start.1 = (bf16[512,256]{1,0:T(8,128)(2,1)S(1)}, bf16[512,256]{1,0:T(8,128)(2,1)S(1)}, u32[]{:S(2)}, u32[]{:S(2)}) collective-permute-start(bf16[512,256]{1,0:T(8,128)(2,1)S(1)} %get-tuple-element.10), channel_id=1, source_target_pairs={{0,2},{1,3},{2,4},{3,5},{4,6},{5,7},{6,0},{7,1},{8,10},{9,11},{10,... | collective-permute-start | bytes 786440 | tf_op jit(solution)/shard_map/ppermute | solution.py:113
  207.9 15.0 %collective-permute-start.2 = (bf16[512,256]{1,0:T(8,128)(2,1)S(1)}, bf16[512,256]{1,0:T(8,128)(2,1)S(1)}, u32[]{:S(2)}, u32[]{:S(2)}) collective-permute-start(bf16[512,256]{1,0:T(8,128)(2,1)S(1)} %get-tuple-element.11), channel_id=1, source_target_pairs={{0,4},{1,5},{2,6},{3,7},{4,0},{5,1},{6,2},{7,3},{8,12},{9,13},{10,... | collective-permute-start | bytes 786440 | tf_op jit(solution)/shard_map/ppermute | solution.py:113
  210.6 12.3 %collective-permute-start.3 = (bf16[512,256]{1,0:T(8,128)(2,1)S(1)}, bf16[512,256]{1,0:T(8,128)(2,1)S(1)}, u32[]{:S(2)}, u32[]{:S(2)}) collective-permute-start(bf16[512,256]{1,0:T(8,128)(2,1)S(1)} %get-tuple-element.12), channel_id=1, source_target_pairs={{0,6},{1,7},{2,0},{3,1},{4,2},{5,3},{6,4},{7,5},{8,14},{9,15},{10,... | collective-permute-start | bytes 786440 | tf_op jit(solution)/shard_map/ppermute | solution.py:113
  223.6 15.6 %all-to-all-start.3 = ((bf16[16,32,256]{2,1,0:T(8,128)(2,1)}), bf16[16,32,256]{2,1,0:T(8,128)(2,1)S(1)}, u32[]{:S(2)}, u32[]{:S(2)}) async-start(bf16[16,32,256]{2,1,0:T(8,128)(2,1)} %bitcast.11), calls=%async_computation.4 | async-start | bytes 524288 | tf_op jit(solution)/shard_map/all_to_all | solution.py:128
Sparse Core Ops, SparseCore 0:
  148.0 49.8 reduce-scatter.1

commit v6 on v4

--- a/solution.py
+++ b/solution.py
@@ -32,7 +32,7 @@
 
 def place(slot, amplitudes, count):
     rows, depth = amplitudes.shape
-    size = 256
+    size = 512
     return pl.pallas_call(
         place_body,
         grid=(count // size,),

time: 247 us -> 247 us (level)
  no operation moved by 1% of the time
where the time goes in v6:
time: 247 us; the launch traced here: 246 us
  blocking collectives  104 us (42%)
  waiting for transfers between devices  47.4 us (19%)
  Pallas kernels  47.2 us (19%)
  starting transfers between devices  20.1 us (8%)
  between operations  13.6 us (6%)
  local copies, waits for them, and re-layouts  8.17 us (3%)
  matrix products  3.98 us (2%)
    all_to_all x1, blocking collectives, exchange(): return lax.all_to_all(x, 'vp', split_axis=0, concat_axis=0, tiled=True)  104 us
    all_to_all x3, waiting for transfers between devices, exchange(): return lax.all_to_all(x, 'vp', split_axis=0, concat_axis=0, tiled=True)  36.6 us
    pallas_call x2, Pallas kernels, multiply(): pl.pallas_call(multiply_body, grid=(count // size,), in_specs=[pl.BlockSp...  33 us
    all_to_all x3, starting transfers between devices, exchange(): return lax.all_to_all(x, 'vp', split_axis=0, concat_axis=0, tiled=True)  14.8 us
    pallas_call x2, Pallas kernels, place(): pl.pallas_call(place_body, grid=(count // size,), in_specs=[pl.BlockSpec(...  13 us
    ppermute x4, waiting for transfers between devices, permute(): return lax.ppermute(x, 'op', list(enumerate(to)))  10.8 us
    unnamed x8, local copies, waits for them, and re-layouts  5.7 us
    ppermute x4, starting transfers between devices, permute(): return lax.ppermute(x, 'op', list(enumerate(to)))  5.25 us
  transfers between devices with their start and end apart: 8, of which 4 were waited for; matrix products, arithmetic and copies ran while one was open for 2% of the time, Pallas kernels for 6%

profile of v6, /device:TPU:0, one launch (start us, length us, event | category | flops | bytes accessed | tf_op | source)
XLA Modules:
  0.0 246.4 jit_solution(3342715638679033919)
XLA Ops:
  6.5 1.1 fusion.9
  8.4 2.2 copy-done
  10.6 9.3 %shard_map.37 = bf16[2048,2048]{1,0:T(8,128)(2,1)S(1)} custom-call(s32[1,1024]{1,0:T(1,128)S(1)} %get-tuple-element.24.slot, bf16[1024,2048]{1,0:T(8,128)(2,1)S(1)} %copy-done), custom_call_target="tpu_custom_call" | custom-call | flops 8589934592 | bytes 12582912 | tf_op jit(solution)/shard_map/pallas_call | solution.py:36
  19.9 103.8 %all_to_all.46 = bf16[16,128,2048]{2,1,0:T(8,128)(2,1)} all-to-all(bf16[16,128,2048]{2,1,0:T(8,128)(2,1)S(1)} %bitcast.23), channel_id=1, replica_groups=mesh['vp'=16,'op'=8] {'vp'}, dimensions={0} | all-to-all | bytes 16777216 | tf_op jit(solution)/shard_map/all_to_all | solution.py:128
  123.7 23.5 %shard_map.38 = bf16[2048,2048]{1,0:T(8,128)(2,1)} custom-call(bf16[2048,2048]{1,0:T(8,128)(2,1)} %bitcast.24, bf16[2048,2048]{1,0:T(8,128)(2,1)} %bitcast.32), custom_call_target="tpu_custom_call" | custom-call | flops 17179869184 | bytes 25165824 | tf_op jit(solution)/shard_map/pallas_call | solution.py:60
  147.3 2.2 copy-done.1
  149.4 3.7 %shard_map.39 = bf16[512,2048]{1,0:T(8,128)(2,1)} custom-call(s32[1,1024]{1,0:T(1,128)S(1)} %get-tuple-element.23.slot, bf16[1024,2048]{1,0:T(8,128)(2,1)S(1)} %copy-done.1), custom_call_target="tpu_custom_call" | custom-call | flops 2147483648 | bytes 6291456 | tf_op jit(solution)/shard_map/pallas_call | solution.py:36
  153.1 3.7 %all-to-all-start.2 = ((bf16[16,32,2048]{2,1,0:T(8,128)(2,1)}), bf16[16,32,2048]{2,1,0:T(8,128)(2,1)S(1)}, u32[]{:S(2)}, u32[]{:S(2)}) async-start(bf16[16,32,2048]{2,1,0:T(8,128)(2,1)} %bitcast.9), calls=%async_computation.3 | async-start | bytes 4194304 | tf_op jit(solution)/shard_map/all_to_all | solution.py:128
  157.0 29.5 %all-to-all-done.2 = bf16[16,32,2048]{2,1,0:T(8,128)(2,1)S(1)} async-done(((bf16[16,32,2048]{2,1,0:T(8,128)(2,1)}), bf16[16,32,2048]{2,1,0:T(8,128)(2,1)S(1)}, u32[]{:S(2)}, u32[]{:S(2)}) %all-to-all-start.2) | async-done | bytes 2097184 | tf_op jit(solution)/shard_map/all_to_all | solution.py:128
  186.5 1.3 copy-done.2
  187.8 9.5 %shard_map.40 = bf16[512,2048]{1,0:T(8,128)(2,1)} custom-call(bf16[512,2048]{1,0:T(8,128)(2,1)} %bitcast.25, bf16[2048,2048]{1,0:T(8,128)(2,1)} %bitcast.33), custom_call_target="tpu_custom_call" | custom-call | flops 4294967296 | bytes 12582912 | tf_op jit(solution)/shard_map/pallas_call | solution.py:60
  197.3 2.5 %constant_dynamic-slice_fusion.2 = (bf16[512,256]{1,0:T(8,128)(2,1)S(1)}, bf16[512,256]{1,0:T(8,128)(2,1)S(1)}, bf16[512,256]{1,0:T(8,128)(2,1)S(1)}, bf16[512,2...) fusion(bf16[512,2048]{1,0:T(8,128)(2,1)} %shard_map.40, ...), kind=kLoop, calls=%fused_computation.27 | loop fusion | bytes 4194336 | tf_op jit(solution)/shard_map/dynamic_slice | solution.py:107
  200.1 4.2 %all-to-all-start.1 = ((bf16[16,128,256]{2,1,0:T(8,128)(2,1)}), bf16[16,128,256]{2,1,0:T(8,128)(2,1)S(1)}, u32[]{:S(2)}, u32[]{:S(2)}) async-start(bf16[16,128,256]{2,1,0:T(8,128)(2,1)} %bitcast.26), calls=%async_computation.2 | async-start | bytes 2097152 | tf_op jit(solution)/shard_map/all_to_all | solution.py:128
  204.3 1.2 pad_maximum_fusion.refs_0_
  205.9 1.0 collective-permute-start.1
  206.9 2.7 %collective-permute-start.2 = (bf16[512,256]{1,0:T(8,128)(2,1)S(1)}, bf16[512,256]{1,0:T(8,128)(2,1)S(1)}, u32[]{:S(2)}, u32[]{:S(2)}) collective-permute-start(bf16[512,256]{1,0:T(8,128)(2,1)S(1)} %get-tuple-element.11), channel_id=1, source_target_pairs={{0,4},{1,5},{2,6},{3,7},{4,0},{5,1},{6,2},{7,3},{8,12},{9,13},{10,... | collective-permute-start | bytes 786440 | tf_op jit(solution)/shard_map/ppermute | solution.py:113
  209.5 1.5 collective-permute-start.3
  211.1 4.2 %collective-permute-done.1.refs_1_ = bf16[512,256]{1,0:T(8,128)(2,1)S(1)} collective-permute-done((bf16[512,256]{1,0:T(8,128)(2,1)S(1)}, bf16[512,256]{1,0:T(8,128)(2,1)S(1)}, u32[]{:S(2)}, u32[]{:S(2)}) %collective-permute-start.1) | collective-permute-done | bytes 262176 | tf_op jit(solution)/shard_map/ppermute | solution.py:113
  215.3 6.5 %collective-permute-done.2.refs_2_ = bf16[512,256]{1,0:T(8,128)(2,1)S(1)} collective-permute-done((bf16[512,256]{1,0:T(8,128)(2,1)S(1)}, bf16[512,256]{1,0:T(8,128)(2,1)S(1)}, u32[]{:S(2)}, u32[]{:S(2)}) %collective-permute-start.2) | collective-permute-done | bytes 262176 | tf_op jit(solution)/shard_map/ppermute | solution.py:113
  221.8 0.8 shard_map.42
  222.6 6.9 %all-to-all-start.3 = ((bf16[16,32,256]{2,1,0:T(8,128)(2,1)}), bf16[16,32,256]{2,1,0:T(8,128)(2,1)S(1)}, u32[]{:S(2)}, u32[]{:S(2)}) async-start(bf16[16,32,256]{2,1,0:T(8,128)(2,1)} %bitcast.11), calls=%async_computation.4 | async-start | bytes 524288 | tf_op jit(solution)/shard_map/all_to_all | solution.py:128
  229.5 1.5 fusion
  231.0 7.1 %all-to-all-done.3 = bf16[16,32,256]{2,1,0:T(8,128)(2,1)S(1)} async-done(((bf16[16,32,256]{2,1,0:T(8,128)(2,1)}), bf16[16,32,256]{2,1,0:T(8,128)(2,1)S(1)}, u32[]{:S(2)}, u32[]{:S(2)}) %all-to-all-start.3) | async-done | bytes 262176 | tf_op jit(solution)/shard_map/all_to_all | solution.py:128
  238.2 1.3 fusion.5
  (16 shorter events, 1.3 us)
Async XLA Ops:
  6.5 193.5 %reduce-scatter.2.cloned.1.call-start = ((), (), s32[]{:S(2)}) async-start(), calls=%async_computation.5 | async-start | bytes 9437184 | tf_op jit(solution)/shard_map/reduce_scatter | solution.py:137
  8.4 2.2 copy-start
  147.2 2.2 copy-start.1
  153.1 33.3 %all-to-all-start.2 = ((bf16[16,32,2048]{2,1,0:T(8,128)(2,1)}), bf16[16,32,2048]{2,1,0:T(8,128)(2,1)S(1)}, u32[]{:S(2)}, u32[]{:S(2)}) async-start(bf16[16,32,2048]{2,1,0:T(8,128)(2,1)} %bitcast.9), calls=%async_computation.3 | async-start | bytes 4194304 | tf_op jit(solution)/shard_map/all_to_all | solution.py:128
  186.5 1.3 copy-start.2
  199.9 5.6 %collective-permute-start = (bf16[512,1024]{1,0:T(8,128)(2,1)S(1)}, bf16[512,1024]{1,0:T(8,128)(2,1)S(1)}, u32[]{:S(2)}, u32[]{:S(2)}) collective-permute-start(bf16[512,1024]{1,0:T(8,128)(2,1)S(1)} %pad_maximum_fusion.1), channel_id=1, source_target_pairs={{0,1},{1,0},{2,3},{3,2},{4,5},{5,4},{6,7},{7,6},{8,9},{9,8},{10,11... | collective-permute-start | bytes 3145736 | tf_op jit(solution)/shard_map/ppermute | solution.py:113
  200.1 22.5 %all-to-all-start.1 = ((bf16[16,128,256]{2,1,0:T(8,128)(2,1)}), bf16[16,128,256]{2,1,0:T(8,128)(2,1)S(1)}, u32[]{:S(2)}, u32[]{:S(2)}) async-start(bf16[16,128,256]{2,1,0:T(8,128)(2,1)} %bitcast.26), calls=%async_computation.2 | async-start | bytes 2097152 | tf_op jit(solution)/shard_map/all_to_all | solution.py:128
  204.3 6.7 %copy-start.3 = (s32[1024,1]{0,1:T(1,128)S(1)}, s32[1024,1]{0,1:T(1,128)}, u32[]{:S(2)}) copy-start(s32[1024,1]{0,1:T(1,128)} %param.5) | copy-start | bytes 12292
  205.9 9.4 %collective-permute-start.1 = (bf16[512,256]{1,0:T(8,128)(2,1)S(1)}, bf16[512,256]{1,0:T(8,128)(2,1)S(1)}, u32[]{:S(2)}, u32[]{:S(2)}) collective-permute-start(bf16[512,256]{1,0:T(8,128)(2,1)S(1)} %get-tuple-element.10), channel_id=1, source_target_pairs={{0,2},{1,3},{2,4},{3,5},{4,6},{5,7},{6,0},{7,1},{8,10},{9,11},{10,... | collective-permute-start | bytes 786440 | tf_op jit(solution)/shard_map/ppermute | solution.py:113
  206.9 14.9 %collective-permute-start.2 = (bf16[512,256]{1,0:T(8,128)(2,1)S(1)}, bf16[512,256]{1,0:T(8,128)(2,1)S(1)}, u32[]{:S(2)}, u32[]{:S(2)}) collective-permute-start(bf16[512,256]{1,0:T(8,128)(2,1)S(1)} %get-tuple-element.11), channel_id=1, source_target_pairs={{0,4},{1,5},{2,6},{3,7},{4,0},{5,1},{6,2},{7,3},{8,12},{9,13},{10,... | collective-permute-start | bytes 786440 | tf_op jit(solution)/shard_map/ppermute | solution.py:113
  209.5 12.3 %collective-permute-start.3 = (bf16[512,256]{1,0:T(8,128)(2,1)S(1)}, bf16[512,256]{1,0:T(8,128)(2,1)S(1)}, u32[]{:S(2)}, u32[]{:S(2)}) collective-permute-start(bf16[512,256]{1,0:T(8,128)(2,1)S(1)} %get-tuple-element.12), channel_id=1, source_target_pairs={{0,6},{1,7},{2,0},{3,1},{4,2},{5,3},{6,4},{7,5},{8,14},{9,15},{10,... | collective-permute-start | bytes 786440 | tf_op jit(solution)/shard_map/ppermute | solution.py:113
  222.6 15.6 %all-to-all-start.3 = ((bf16[16,32,256]{2,1,0:T(8,128)(2,1)}), bf16[16,32,256]{2,1,0:T(8,128)(2,1)S(1)}, u32[]{:S(2)}, u32[]{:S(2)}) async-start(bf16[16,32,256]{2,1,0:T(8,128)(2,1)} %bitcast.11), calls=%async_computation.4 | async-start | bytes 524288 | tf_op jit(solution)/shard_map/all_to_all | solution.py:128
Sparse Core Ops, SparseCore 0:
  147.4 49.8 reduce-scatter.1
